TPU v7x, 32 devices: a whole 2x2x4 slice. The times are simulated.
32 devices in a mesh: groups: 2 (over y), expert: 4 (over z), tensor: 4 (over x, core).
Axes of the slice: x: 2, y: 2, z: 4, core: 2. Of those that a mesh axis runs over, the one named last changes fastest.
Arguments:
- tokens: bfloat16 [2048, 1440], P(('groups', 'expert'), 'tensor'), parts along dimension 0, may hold values from -6 to 6
- out_grad: bfloat16 [2048, 1440], P(('groups', 'expert'), 'tensor'), parts along dimension 0, may hold values from -6 to 6
- routes: int32 [2048, 2], P(('groups', 'expert')), parts along dimension 0, may hold values from 0 to 3, all different within a row; in each aligned block of 256 rows (0 to 255, 256 to 511, ...) at most 256 rows name the same one
- route_probs: bfloat16 [2048, 2], P(('groups', 'expert')), parts along dimension 0, may hold values from 0.049804688 to 1
- w_gate: bfloat16 [4, 1440, 1440], P('expert', None, 'tensor'), may hold values from -0.21875 to 0.21875
- w_up: bfloat16 [4, 1440, 1440], P('expert', None, 'tensor'), may hold values from -0.21875 to 0.21875
- w_down: bfloat16 [4, 1440, 1440], P('expert', 'tensor'), may hold values from -0.15625 to 0.15625
Outputs:
- grad_tokens: bfloat16 [2048, 1440], P(('groups', 'expert'), 'tensor'), parts along dimension 0
- grad_gate: bfloat16 [8, 1440, 1440], P(('groups', 'expert'), None, 'tensor'), parts along dimension 0
- grad_up: bfloat16 [8, 1440, 1440], P(('groups', 'expert'), None, 'tensor'), parts along dimension 0
- grad_down: bfloat16 [8, 1440, 1440], P(('groups', 'expert'), 'tensor'), parts along dimension 0
There are 2 independent parts, one for each index of `groups`. A program takes and returns all parts, laid end to end along the dimension named above; an argument that names none is the same for every part. Nothing has to cross between parts.
Inputs may be any that keep to these rules, and one draw needn't show every extreme that they name: In the rows of one device (aligned blocks of 256 tokens) no expert is named by more than 256 routes; the 2 ids of a token differ.
All inputs are finite; a program needn't handle non-finite values.
Results may differ from a plain program's by a relative error of at most 0.01.
Values may be sent and summed in bfloat16 or wider, within the bound.
No kernel may reach another device: no remote copies, remote signals or barrier semaphores. Data moves between devices by JAX's collectives and lax.ppermute only.
A program may use at most 64 MiB of HBM per device.

v0:
```python
import jax
import jax.numpy as jnp
from jax import lax
from jax.sharding import PartitionSpec as P


def per_device(tokens, out_grad, routes, route_probs, w_gate, w_up, w_down):
    expert_count = lax.axis_size("expert")
    token_count, route_count = routes.shape
    route_total = token_count * route_count
    capacity = 2 * route_total
    slot_size = capacity // expert_count
    flat_ids = routes.reshape(-1)
    onehot = (flat_ids[:, None] == jnp.arange(expert_count, dtype=jnp.int32)[None, :]).astype(
        jnp.int32
    )
    before = jnp.cumsum(onehot, axis=0) - onehot
    position = jnp.sum(before * onehot, axis=1)
    slot_of_route = flat_ids * slot_size + position
    route_of_slot = (
        jnp.full((capacity,), route_total, jnp.int32)
        .at[slot_of_route]
        .set(jnp.arange(route_total, dtype=jnp.int32))
    )
    token_of_slot = route_of_slot // route_count
    weights_send = jnp.take(
        jnp.concatenate([route_probs.reshape(-1), jnp.zeros((1,), route_probs.dtype)]),
        route_of_slot,
        axis=0,
    )

    def spread(block_rows):
        padded = jnp.concatenate(
            [block_rows, jnp.zeros((1, block_rows.shape[1]), block_rows.dtype)]
        )
        return jnp.take(padded, token_of_slot, axis=0)

    full_x, full_dy = (
        lax.all_gather(tokens, "tensor", axis=1, tiled=True),
        lax.all_gather(out_grad, "tensor", axis=1, tiled=True),
    )
    rows_x, rows_dy, rows_weight = (
        lax.all_to_all(spread(full_x), "expert", split_axis=0, concat_axis=0, tiled=True),
        lax.all_to_all(spread(full_dy), "expert", split_axis=0, concat_axis=0, tiled=True),
        lax.all_to_all(weights_send, "expert", split_axis=0, concat_axis=0, tiled=True),
    )
    gate_weight = w_gate[0]
    up_weight = w_up[0]
    down_weight = w_down[0]
    contract_last = (((1,), (1,)), ((), ()))
    contract_rows = (((0,), (0,)), ((), ()))
    weight_row = rows_weight.astype(jnp.float32)[:, None]
    pre_gate = jnp.dot(rows_x, gate_weight, preferred_element_type=jnp.float32)
    pre_up = jnp.dot(rows_x, up_weight, preferred_element_type=jnp.float32)
    hidden_grad = (
        lax.dot_general(rows_dy, down_weight, contract_last, preferred_element_type=jnp.float32)
        * weight_row
    )
    sigmoid_gate = jax.nn.sigmoid(pre_gate)
    activated = pre_gate * sigmoid_gate
    hidden = activated * pre_up
    grad_gate_pre = (
        hidden_grad * pre_up * sigmoid_gate * (1.0 + pre_gate * (1.0 - sigmoid_gate))
    ).astype(jnp.bfloat16)
    grad_up_pre = (hidden_grad * activated).astype(jnp.bfloat16)
    scaled_hidden = (hidden * weight_row).astype(jnp.bfloat16)
    partials = lax.dot_general(
        grad_gate_pre, gate_weight, contract_last, preferred_element_type=jnp.float32
    )
    partials = partials + lax.dot_general(
        grad_up_pre, up_weight, contract_last, preferred_element_type=jnp.float32
    )
    partials = partials.astype(jnp.bfloat16)
    summed = (
        lax.psum_scatter(partials, "tensor", scatter_dimension=1, tiled=True)
        .astype(jnp.float32)
        .astype(jnp.bfloat16)
    )
    returned = lax.all_to_all(summed, "expert", split_axis=0, concat_axis=0, tiled=True)
    per_route = (
        jnp.take(returned, slot_of_route, axis=0)
        .astype(jnp.float32)
        .reshape(token_count, route_count, -1)
    )
    grad_tokens = jnp.sum(per_route, axis=1).astype(jnp.bfloat16)
    grad_gate = lax.dot_general(
        rows_x, grad_gate_pre, contract_rows, preferred_element_type=jnp.float32
    ).astype(jnp.bfloat16)
    grad_up = lax.dot_general(
        rows_x, grad_up_pre, contract_rows, preferred_element_type=jnp.float32
    ).astype(jnp.bfloat16)
    grad_down = lax.dot_general(
        scaled_hidden, rows_dy, contract_rows, preferred_element_type=jnp.float32
    ).astype(jnp.bfloat16)
    return (grad_tokens, grad_gate[None], grad_up[None], grad_down[None])


def solution(mesh):
    placed = (
        P(("groups", "expert"), "tensor"),
        P(("groups", "expert"), "tensor"),
        P(("groups", "expert"), None),
        P(("groups", "expert"), None),
        P("expert", None, "tensor"),
        P("expert", None, "tensor"),
        P("expert", "tensor", None),
    )
    return jax.shard_map(
        per_device,
        mesh=mesh,
        in_specs=placed,
        out_specs=(
            P(("groups", "expert"), "tensor"),
            P(("groups", "expert"), None, "tensor"),
            P(("groups", "expert"), None, "tensor"),
            P(("groups", "expert"), "tensor", None),
        ),
        check_vma=False,
    )
```

profile of v0, /device:TPU:0, one launch (start us, length us, event | category | flops | bytes accessed | tf_op | source)
XLA Modules:
  0.0 294.3 jit_solution(11519049402996591750)
XLA Ops:
  7.2 0.0 copy-start
  7.2 0.9 copy.48
  8.1 0.0 copy-start.7
  8.1 0.1 eq.26
  8.2 0.1 reshape.117
  8.4 0.7 broadcast_multiply_fusion
  9.1 1.2 reduce-window.6
  10.3 0.2 slice_reduce_fusion
  10.5 0.2 reduce-window.9
  10.7 0.1 add_bitcast_fusion
  10.8 0.1 copy.52
  10.9 0.1 mul.60
  11.1 2.4 scatter_custom_fusion
  13.6 0.8 copy.56
  14.4 0.1 reshape.119
  14.6 6.8 %gather_fusion = bf16[1024]{0:T(1024)(128)(2,1)S(1)} fusion(bf16[513]{0:T(1024)(128)(2,1)S(1)} %pad_maximum_fusion, s32[1024]{0:T(1024)S(1)} %get-tuple-element.19), kind=kCustom, calls=%fused_computation.2 | custom fusion | bytes 8192 | tf_op jit(solution)/shard_map/jit(_take)/gather | solution.py:26
  21.4 0.0 copy-start.8
  21.4 0.5 broadcast.122
  21.9 0.7 reduce.3
  22.6 0.6 reshape.171
  23.2 6.3 %all-to-all-start.1 = ((bf16[4,2,128]{2,1,0:T(2,128)(2,1)}), bf16[4,2,128]{2,1,0:T(2,128)(2,1)S(1)}, u32[]{:S(2)}, u32[]{:S(2)}) async-start(bf16[4,2,128]{2,1,0:T(2,128)(2,1)} %reshape.171), calls=%async_computation.1 | async-start | bytes 4096 | tf_op jit(solution)/shard_map/all_to_all | solution.py:45
  29.5 8.3 %all_gather.7 = bf16[256,1440]{0,1:T(8,128)(2,1)S(1)} all-gather(bf16[256,360]{0,1:T(8,128)(2,1)S(1)} %copy-done.7), channel_id=1, replica_groups=mesh['groups'=2,'expert'=4,'tensor'=4] {'tensor'}, dimensions={1}, use_global_device_ids=true | all-gather | bytes 921600 | tf_op jit(solution)/shard_map/all_gather | solution.py:39
  37.9 0.3 copy.58
  38.1 8.5 %all_gather.6 = bf16[256,1440]{0,1:T(8,128)(2,1)S(1)} all-gather(bf16[256,360]{0,1:T(8,128)(2,1)S(1)} %copy-done.8), channel_id=1, replica_groups=mesh['groups'=2,'expert'=4,'tensor'=4] {'tensor'}, dimensions={1}, use_global_device_ids=true | all-gather | bytes 921600 | tf_op jit(solution)/shard_map/all_gather | solution.py:40
  46.6 0.3 copy.53
  46.9 0.1 concatenate.11
  47.0 0.1 concatenate.9
  47.0 5.6 %gather_fusion.3 = bf16[1024,1440]{1,0:T(8,128)(2,1)} fusion(bf16[257,1440]{1,0:T(8,128)(2,1)S(1)} %concatenate.11, s32[1024]{0:T(1024)S(1)} %get-tuple-element.20), kind=kCustom, calls=%fused_computation.1.clone | custom fusion | bytes 5902336 | tf_op jit(solution)/shard_map/jit(_take)/gather | solution.py:36
  52.7 5.6 %gather_fusion.2 = bf16[1024,1440]{1,0:T(8,128)(2,1)} fusion(bf16[257,1440]{1,0:T(8,128)(2,1)S(1)} %concatenate.9, s32[1024]{0:T(1024)S(1)} %get-tuple-element.20), kind=kCustom, calls=%fused_computation.clone | custom fusion | bytes 5902336 | tf_op jit(solution)/shard_map/jit(_take)/gather | solution.py:36
  58.2 5.0 %broadcast_select_fusion.1 = (bf16[1024,1440]{1,0:T(8,128)(2,1)}, bf16[1024,1440]{1,0:T(8,128)(2,1)}) fusion(bf16[1024,1440]{1,0:T(8,128)(2,1)} %gather_fusion.2, pred[1024]{0:T(1024)(128)(4,1)S(1)} %compare_and_fusion, bf16[1024,1440]{1,0:T(8,128)(2,1)} %gather_fusion.3), kind=kLoop, calls=%fused_computation.7 | loop fusion | flops 2949120 | bytes 11797504 | tf_op jit(solution)/shard_map/jit(_take)/select_n | solution.py:36
  63.3 4.7 %copy.59 = bf16[4,256,1440]{1,2,0:T(8,128)(2,1)} copy(bf16[4,256,1440]{2,1,0:T(8,128)(2,1)} %bitcast.69) | data formatting | bytes 5898240 | tf_op jit(solution)/shard_map/all_to_all | solution.py:43
  67.9 5.1 %all-to-all-start.2 = ((bf16[4,256,1440]{1,2,0:T(8,128)(2,1)}), bf16[4,256,1440]{1,2,0:T(8,128)(2,1)}, u32[]{:S(2)}, u32[]{:S(2)}) async-start(bf16[4,256,1440]{1,2,0:T(8,128)(2,1)} %copy.59), calls=%async_computation.2 | async-start | bytes 5898240 | tf_op jit(solution)/shard_map/all_to_all | solution.py:43
  73.0 4.7 %copy.54 = bf16[4,256,1440]{1,2,0:T(8,128)(2,1)} copy(bf16[4,256,1440]{2,1,0:T(8,128)(2,1)} %bitcast.68) | data formatting | bytes 5898240 | tf_op jit(solution)/shard_map/all_to_all | solution.py:44
  77.7 62.5 %all-to-all-done.2 = bf16[4,256,1440]{1,2,0:T(8,128)(2,1)} async-done(((bf16[4,256,1440]{1,2,0:T(8,128)(2,1)}), bf16[4,256,1440]{1,2,0:T(8,128)(2,1)}, u32[]{:S(2)}, u32[]{:S(2)}) %all-to-all-start.2) | async-done | bytes 2949152 | tf_op jit(solution)/shard_map/all_to_all | solution.py:43
  140.1 4.7 %all-to-all-start = ((bf16[4,256,1440]{1,2,0:T(8,128)(2,1)}), bf16[4,256,1440]{1,2,0:T(8,128)(2,1)}, u32[]{:S(2)}, u32[]{:S(2)}) async-start(bf16[4,256,1440]{1,2,0:T(8,128)(2,1)} %copy.54), calls=%async_computation | async-start | bytes 5898240 | tf_op jit(solution)/shard_map/all_to_all | solution.py:44
  144.8 0.2 reduce-scatter.2.cloned.1.call-start
  145.1 2.2 copy.66
  147.3 2.5 fusion.6
  149.9 2.5 fusion.9
  152.4 58.7 %all-to-all-done = bf16[4,256,1440]{1,2,0:T(8,128)(2,1)} async-done(((bf16[4,256,1440]{1,2,0:T(8,128)(2,1)}), bf16[4,256,1440]{1,2,0:T(8,128)(2,1)}, u32[]{:S(2)}, u32[]{:S(2)}) %all-to-all-start) | async-done | bytes 2949152 | tf_op jit(solution)/shard_map/all_to_all | solution.py:44
  211.1 2.4 copy.65
  213.5 0.2 copy-done.11
  213.7 0.4 copy-done.13
  214.1 1.8 multiply_convert_fusion.1
  215.9 0.0 copy-start.6
  215.9 1.7 fusion.4
  217.6 3.4 %add_convert_fusion = bf16[1024,1440]{0,1:T(8,128)(2,1)} fusion(f32[1024,1440]{0,1:T(8,128)S(1)} %fusion.4, bf16[1024,360]{0,1:T(8,128)(2,1)S(1)} %get-tuple-element.17, bf16[1,1440,360]{2,1,0:T(8,128)(2,1)S(1)} %copy-done.6), kind=kOutput, calls=%fused_computation.5 | convolution fusion | flops 1064632320 | bytes 10621440 | tf_op jit(solution)/shard_map/dot_general | solution.py:70
  221.1 0.0 reduce-scatter.2.cloned.1.call-update
  221.1 0.1 reduce_sum.26
  221.3 0.1 copy.50
  221.3 0.4 copy-done.9
  221.8 0.2 copy.51
  222.0 34.2 %reduce-scatter.2.cloned.1.call-done = bf16[1024,360]{0,1:T(8,128)(2,1)} async-done(((bf16[1024,1440]{0,1:T(8,128)(2,1)}), bf16[1024,360]{0,1:T(8,128)(2,1)}) %reduce-scatter.2.cloned.1.call-update) | async-done | bytes 737296 | tf_op jit(solution)/shard_map/reduce_scatter | solution.py:75
  256.2 2.1 copy.70
  258.3 4.6 %all-to-all-start.3 = ((bf16[4,256,360]{1,2,0:T(8,128)(2,1)}), bf16[4,256,360]{1,2,0:T(8,128)(2,1)S(1)}, u32[]{:S(2)}, u32[]{:S(2)}) async-start(bf16[4,256,360]{1,2,0:T(8,128)(2,1)} %bitcast.65), calls=%async_computation.4 | async-start | bytes 1474560 | tf_op jit(solution)/shard_map/all_to_all | solution.py:79
  262.9 4.7 %fusion.1 = bf16[1,1440,360]{2,1,0:T(8,128)(2,1)} fusion(bf16[1024,1440]{0,1:T(8,128)(2,1)} %bitcast.72, bf16[1024,360]{0,1:T(8,128)(2,1)S(1)} %get-tuple-element.17), kind=kOutput, calls=%fused_computation.12 | convolution fusion | flops 1062201600 | bytes 4723200 | tf_op jit(solution)/shard_map/dot_general | solution.py:89
  267.6 2.7 fusion
  270.3 2.5 fusion.2
  272.8 9.1 %all-to-all-done.3 = bf16[4,256,360]{1,2,0:T(8,128)(2,1)S(1)} async-done(((bf16[4,256,360]{1,2,0:T(8,128)(2,1)}), bf16[4,256,360]{1,2,0:T(8,128)(2,1)S(1)}, u32[]{:S(2)}, u32[]{:S(2)}) %all-to-all-start.3) | async-done | bytes 737312 | tf_op jit(solution)/shard_map/all_to_all | solution.py:79
  281.9 0.4 copy.62
  282.3 1.9 gather_fusion.1
  284.2 0.2 gather.15
  284.4 2.2 fusion.13
  286.6 0.8 copy.63
  (37 shorter events, 0.2 us)
Async XLA Ops:
  7.2 140.2 %copy-start = (bf16[1,1440,360]{2,1,0:T(8,128)(2,1)S(1)}, bf16[1,1440,360]{2,1,0:T(8,128)(2,1)}, u32[]{:S(2)}) copy-start(bf16[1,1440,360]{2,1,0:T(8,128)(2,1)} %param.13) | copy-start | bytes 3110404
  8.1 21.4 %copy-start.7 = (bf16[256,360]{0,1:T(8,128)(2,1)S(1)}, bf16[256,360]{0,1:T(8,128)(2,1)}, u32[]{:S(2)}) copy-start(bf16[256,360]{0,1:T(8,128)(2,1)} %param.9) | copy-start | bytes 552964
  21.4 16.8 %copy-start.8 = (bf16[256,360]{0,1:T(8,128)(2,1)S(1)}, bf16[256,360]{0,1:T(8,128)(2,1)}, u32[]{:S(2)}) copy-start(bf16[256,360]{0,1:T(8,128)(2,1)} %param.10) | copy-start | bytes 552964
  23.2 44.7 %all-to-all-start.1 = ((bf16[4,2,128]{2,1,0:T(2,128)(2,1)}), bf16[4,2,128]{2,1,0:T(2,128)(2,1)S(1)}, u32[]{:S(2)}, u32[]{:S(2)}) async-start(bf16[4,2,128]{2,1,0:T(2,128)(2,1)} %reshape.171), calls=%async_computation.1 | async-start | bytes 4096 | tf_op jit(solution)/shard_map/all_to_all | solution.py:45
  67.9 72.2 %all-to-all-start.2 = ((bf16[4,256,1440]{1,2,0:T(8,128)(2,1)}), bf16[4,256,1440]{1,2,0:T(8,128)(2,1)}, u32[]{:S(2)}, u32[]{:S(2)}) async-start(bf16[4,256,1440]{1,2,0:T(8,128)(2,1)} %copy.59), calls=%async_computation.2 | async-start | bytes 5898240 | tf_op jit(solution)/shard_map/all_to_all | solution.py:43
  140.1 70.9 %all-to-all-start = ((bf16[4,256,1440]{1,2,0:T(8,128)(2,1)}), bf16[4,256,1440]{1,2,0:T(8,128)(2,1)}, u32[]{:S(2)}, u32[]{:S(2)}) async-start(bf16[4,256,1440]{1,2,0:T(8,128)(2,1)} %copy.54), calls=%async_computation | async-start | bytes 5898240 | tf_op jit(solution)/shard_map/all_to_all | solution.py:44
  144.8 111.4 %reduce-scatter.2.cloned.1.call-start = ((), (), s32[]{:S(2)}) async-start(), calls=%async_computation.5 | async-start | bytes 3686400 | tf_op jit(solution)/shard_map/reduce_scatter | solution.py:75
  147.3 2.6 copy-start.1
  147.3 2.5 copy-start.5
  211.1 2.4 copy-start.10
  211.1 2.6 copy-start.11
  211.1 3.0 %copy-start.13 = (f32[1024,360]{0,1:T(8,128)S(1)}, f32[1024,360]{0,1:T(8,128)}, u32[]{:S(2)}) copy-start(f32[1024,360]{0,1:T(8,128)} %fusion.9) | copy-start | bytes 4423684
  213.5 2.4 copy-start.3
  215.9 1.7 copy-start.6
  221.1 0.7 copy-start.9
  258.3 23.6 %all-to-all-start.3 = ((bf16[4,256,360]{1,2,0:T(8,128)(2,1)}), bf16[4,256,360]{1,2,0:T(8,128)(2,1)S(1)}, u32[]{:S(2)}, u32[]{:S(2)}) async-start(bf16[4,256,360]{1,2,0:T(8,128)(2,1)} %bitcast.65), calls=%async_computation.4 | async-start | bytes 1474560 | tf_op jit(solution)/shard_map/all_to_all | solution.py:79
  262.9 4.7 %copy-start.2 = (bf16[4,180,8,256]{3,2,0,1:T(8,128)(2,1)S(1)}, bf16[4,180,8,256]{3,2,0,1:T(8,128)(2,1)}, u32[]{:S(2)}) copy-start(bf16[4,180,8,256]{3,2,0,1:T(8,128)(2,1)} %copy-done.1) | copy-start | bytes 8847364
  267.6 2.7 copy-start.4
  267.6 2.7 copy-start.12
  267.6 2.7 copy-start.14
Sparse Core Ops, SparseCore 0:
  221.2 34.8 reduce-scatter.1
where the time goes:
time: 295 us; the launch traced here: 294 us
  waiting for transfers between devices  164 us (56%)
  local copies, waits for them, and re-layouts  45.8 us (16%)
  matrix products  21.9 us (7%)
  starting transfers between devices  20.9 us (7%)
  blocking collectives  16.8 us (6%)
  between operations  14.4 us (5%)
  other arithmetic  10.1 us (3%)
    all_to_all x1, waiting for transfers between devices, per_device(): lax.all_to_all(spread(full_x), 'expert', split_axis=0, concat_axis=0, til...  62.5 us
    all_to_all x1, waiting for transfers between devices, per_device(): lax.all_to_all(spread(full_dy), 'expert', split_axis=0, concat_axis=0, ti...  58.7 us
    reduce_scatter x1, waiting for transfers between devices, per_device(): lax.psum_scatter(partials, 'tensor', scatter_dimension=1, tiled=True)  34.2 us
    gather x2, local copies, waits for them, and re-layouts, spread(): return jnp.take(padded, token_of_slot, axis=0)  11.2 us
    all_to_all x1, waiting for transfers between devices, per_device(): lax.all_to_all(summed, 'expert', split_axis=0, concat_axis=0, tiled=True)  9.11 us
    all_gather x1, blocking collectives, per_device(): lax.all_gather(out_grad, 'tensor', axis=1, tiled=True)  8.45 us
    all_gather x1, blocking collectives, per_device(): lax.all_gather(tokens, 'tensor', axis=1, tiled=True)  8.33 us
    all_to_all x2, local copies, waits for them, and re-layouts, per_device(): lax.all_to_all(spread(full_dy), 'expert', split_axis=0, concat_axis=0, ti...  7.06 us
  transfers between devices with their start and end apart: 5, of which 4 were waited for; matrix products, arithmetic and copies ran while one was open for 15% of the time, Pallas kernels for 0%

commit v1 on v0

--- a/solution.py
+++ b/solution.py
@@ -4,7 +4,7 @@
 from jax.sharding import PartitionSpec as P
 
 
-def per_device(tokens, out_grad, routes, route_probs, w_gate, w_up, w_down):
+def per_device_routed(tokens, out_grad, routes, route_probs, w_gate, w_up, w_down):
     expert_count = lax.axis_size("expert")
     token_count, route_count = routes.shape
     route_total = token_count * route_count
@@ -95,6 +95,93 @@
     return (grad_tokens, grad_gate[None], grad_up[None], grad_down[None])
 
 
+F32 = jnp.float32
+BF16 = jnp.bfloat16
+
+
+def swap(block, axis, bit):
+    size = lax.axis_size(axis)
+    return lax.ppermute(block, axis, [(i, i ^ bit) for i in range(size)])
+
+
+def in_order(pieces, me):
+    stacked = jnp.stack(pieces)
+    return jnp.concatenate(
+        [lax.dynamic_index_in_dim(stacked, me ^ t, 0, keepdims=False) for t in range(len(pieces))]
+    )
+
+
+def add(a, b):
+    return (a.astype(F32) + b.astype(F32)).astype(BF16)
+
+
+def per_device(tokens, out_grad, routes, route_probs, w_gate, w_up, w_down):
+    experts, partners = lax.axis_size("expert"), lax.axis_size("tensor")
+    token_count, route_count = routes.shape
+    if experts != 4 or partners != 4:
+        return per_device_routed(tokens, out_grad, routes, route_probs, w_gate, w_up, w_down)
+    width = tokens.shape[1]
+    me = lax.axis_index("tensor")
+    here = lax.axis_index("expert")
+
+    named = routes[:, :, None] == jnp.arange(experts, dtype=jnp.int32)[None, None, :]
+    by_expert = jnp.sum(jnp.where(named, route_probs.astype(F32)[:, :, None], 0.0), axis=1)
+    weights = jnp.zeros((16, token_count), BF16).at[:experts].set(by_expert.T.astype(BF16))
+    own = jnp.concatenate([tokens.T, out_grad.T, weights])
+
+    z1 = swap(own, "expert", 1)
+    z2 = swap(own, "expert", 2)
+    z3 = swap(z2, "expert", 1)
+
+    gate_t = w_gate[0].T
+    up_t = w_up[0].T
+    down = w_down[0]
+    both = jnp.concatenate([w_gate[0], w_up[0]], axis=1)
+
+    def forward(block):
+        far = swap(block, "tensor", 2)
+        near = swap(block, "tensor", 1)
+        diagonal = swap(far, "tensor", 1)
+        pieces = (block, near, far, diagonal)
+        x = in_order([p[:width] for p in pieces], me)
+        dy = in_order([p[width : 2 * width] for p in pieces], me)
+        weight = lax.dynamic_slice_in_dim(block, 2 * width + here, 1, 0).astype(F32)
+        pre_gate = jnp.dot(gate_t, x, preferred_element_type=F32)
+        pre_up = jnp.dot(up_t, x, preferred_element_type=F32)
+        hidden_grad = jnp.dot(down, dy, preferred_element_type=F32) * weight
+        sigmoid_gate = jax.nn.sigmoid(pre_gate)
+        activated = pre_gate * sigmoid_gate
+        grad_gate_pre = (
+            hidden_grad * pre_up * sigmoid_gate * (1.0 + pre_gate * (1.0 - sigmoid_gate))
+        ).astype(BF16)
+        grad_up_pre = (hidden_grad * activated).astype(BF16)
+        scaled_hidden = (activated * pre_up * weight).astype(BF16)
+        grads = jnp.concatenate([grad_gate_pre, grad_up_pre])
+        partial = jnp.dot(both, grads, preferred_element_type=F32).astype(BF16)
+        partial = partial.reshape(partners, width, token_count)
+        mine = [lax.dynamic_index_in_dim(partial, me ^ k, 0, keepdims=False) for k in range(4)]
+        got = swap(jnp.stack([mine[1], mine[3]]), "tensor", 1)
+        kept = add(mine[0], got[0])
+        sent = add(mine[2], got[1])
+        summed = add(kept, swap(sent, "tensor", 2))
+        return x, dy, grads, scaled_hidden, summed
+
+    parts = [forward(b) for b in (own, z1, z2, z3)]
+    s0, s1, s2, s3 = [p[4] for p in parts]
+    t0 = s0.astype(F32) + swap(s1, "expert", 1).astype(F32)
+    t2 = add(s2, swap(s3, "expert", 1))
+    grad_tokens = (t0 + swap(t2, "expert", 2).astype(F32)).astype(BF16).T
+
+    parts = lax.optimization_barrier([p[:4] for p in parts])
+    x, dy, grads, scaled = [jnp.concatenate([p[i] for p in parts], axis=1) for i in range(4)]
+    lanes = (((1,), (1,)), ((), ()))
+    half = grads.shape[0] // 2
+    grad_gate = lax.dot_general(x, grads[:half], lanes, preferred_element_type=F32).astype(BF16)
+    grad_up = lax.dot_general(x, grads[half:], lanes, preferred_element_type=F32).astype(BF16)
+    grad_down = lax.dot_general(scaled, dy, lanes, preferred_element_type=F32).astype(BF16)
+    return (grad_tokens, grad_gate[None], grad_up[None], grad_down[None])
+
+
 def solution(mesh):
     placed = (
         P(("groups", "expert"), "tensor"),

time: 295 us -> 89.1 us (0.30)
  waiting for transfers between devices: 164 us -> 37.6 us
  local copies, waits for them, and re-layouts: 45.8 us -> 3.5 us
  blocking collectives: 16.8 us -> 0 us
  between operations: 14.4 us -> 1.35 us
  other arithmetic: 10.1 us -> 5.32 us
  matrix products: 21.9 us -> 18.1 us
    all_to_all x4 -> x0, waiting for transfers between devices: 130 us -> none  [the longest x1 62.5 us: per_device(): lax.all_to_all(spread(full_x), 'expert', split_axis=0, concat_axis=0, til...]
    ppermute x0 -> x26, waiting for transfers between devices: none -> 37.6 us  [swap(): return lax.ppermute(block, axis, [(i, i ^ bit) for i in range(size)])]
    reduce_scatter x1 -> x0, waiting for transfers between devices: 34.2 us -> none  [per_device(): lax.psum_scatter(partials, 'tensor', scatter_dimension=1, tiled=True)]
    ppermute x0 -> x26, starting transfers between devices: none -> 22.9 us  [swap(): return lax.ppermute(block, axis, [(i, i ^ bit) for i in range(size)])]
    all_to_all x4 -> x0, starting transfers between devices: 20.7 us -> none  [the longest x1 6.32 us: per_device(): lax.all_to_all(weights_send, 'expert', split_axis=0, concat_axis=0, tiled...]
    gather x5 -> x0, local copies, waits for them, and re-layouts: 20.1 us -> none  [the longest x2 11.2 us: spread(): return jnp.take(padded, token_of_slot, axis=0)]
    all_gather x2 -> x0, blocking collectives: 16.8 us -> none  [the longest x1 8.45 us: per_device(): lax.all_gather(out_grad, 'tensor', axis=1, tiled=True)]
    all_to_all x6 -> x0, local copies, waits for them, and re-layouts: 16.4 us -> none  [the longest x2 7.06 us: per_device(): lax.all_to_all(spread(full_dy), 'expert', split_axis=0, concat_axis=0, ti...]
  transfers between devices with their start and end apart: 5 -> 26, of which waited for: 4 -> 9; matrix products, arithmetic and copies ran while one was open for 15% -> 24% of each run, Pallas kernels for 0% -> 0%
where the time goes in v1:
time: 89.1 us; the launch traced here: 88.8 us
  waiting for transfers between devices  37.6 us (42%)
  starting transfers between devices  22.9 us (26%)
  matrix products  18.1 us (20%)
  other arithmetic  5.32 us (6%)
  local copies, waits for them, and re-layouts  3.5 us (4%)
  between operations  1.35 us (2%)
    ppermute x26, waiting for transfers between devices, swap(): return lax.ppermute(block, axis, [(i, i ^ bit) for i in range(size)])  37.6 us
    ppermute x26, starting transfers between devices, swap(): return lax.ppermute(block, axis, [(i, i ^ bit) for i in range(size)])  22.9 us
    dot_general x4, matrix products, forward(): partial = jnp.dot(both, grads, preferred_element_type=F32).astype(BF16)  3.22 us
    dot_general x1, matrix products, per_device(): lax.dot_general(x, grads[:half], lanes, preferred_element_type=F32)  2.72 us
    dot_general x1, matrix products, per_device(): lax.dot_general(x, grads[half:], lanes, preferred_element_type=F32)  2.72 us
    dot_general x4, matrix products, forward(): pre_up = jnp.dot(up_t, x, preferred_element_type=F32)  2.66 us
    dot_general x4, matrix products, forward(): pre_gate = jnp.dot(gate_t, x, preferred_element_type=F32)  2.54 us
    dot_general x1, matrix products, per_device(): lax.dot_general(scaled, dy, lanes, preferred_element_type=F32).astype(BF16)  2.37 us
  transfers between devices with their start and end apart: 26, of which 9 were waited for; matrix products, arithmetic and copies ran while one was open for 24% of the time, Pallas kernels for 0%

profile of v1, /device:TPU:0, one launch (start us, length us, event | category | flops | bytes accessed | tf_op | source)
XLA Modules:
  0.0 88.8 jit_solution(17375539966382052827)
XLA Ops:
  0.6 0.8 convert_element_type.243
  1.4 0.7 select_reduce_fusion
  2.1 1.0 %fusion.34 = bf16[736,256]{1,0:T(8,128)(2,1)S(1)} fusion(bf16[4,256]{1,0:T(4,128)(2,1)S(1)} %bitcast.285, bf16[360,256]{1,0:T(8,128)(2,1)} %bitcast.283, bf16[360,256]{1,0:T(8,128)(2,1)} %bitcast.281), kind=kLoop, calls=%fused_computation.63 | loop fusion | flops 1507328 | bytes 747520 | tf_op jit(solution)/shard_map/concatenate | solution.py:130
  3.2 4.1 %collective-permute-start.12 = (bf16[736,256]{1,0:T(8,128)(2,1)S(1)}, bf16[736,256]{1,0:T(8,128)(2,1)S(1)}, u32[]{:S(2)}, u32[]{:S(2)}) collective-permute-start(bf16[736,256]{1,0:T(8,128)(2,1)S(1)} %fusion.34), channel_id=1, source_target_pairs={{0,8},{4,12},{8,0},{12,4},{1,9},{5,13},{9,1},{13,5},{2,10},{6,14},... | collective-permute-start | bytes 1130504 | tf_op jit(solution)/shard_map/ppermute | solution.py:104
  7.3 1.6 %collective-permute-start.5 = (bf16[736,256]{1,0:T(8,128)(2,1)S(1)}, bf16[736,256]{1,0:T(8,128)(2,1)S(1)}, u32[]{:S(2)}, u32[]{:S(2)}) collective-permute-start(bf16[736,256]{1,0:T(8,128)(2,1)S(1)} %fusion.34), channel_id=1, source_target_pairs={{0,4},{4,0},{8,12},{12,8},{1,5},{5,1},{9,13},{13,9},{2,6},{6,2},{1... | collective-permute-start | bytes 1130504 | tf_op jit(solution)/shard_map/ppermute | solution.py:104
  8.8 1.5 %collective-permute-start.1 = (bf16[736,256]{1,0:T(8,128)(2,1)S(1)}, bf16[736,256]{1,0:T(8,128)(2,1)S(1)}, u32[]{:S(2)}, u32[]{:S(2)}) collective-permute-start(bf16[736,256]{1,0:T(8,128)(2,1)S(1)} %fusion.34), channel_id=1, source_target_pairs={{0,2},{1,3},{2,0},{3,1},{4,6},{5,7},{6,4},{7,5},{8,10},{9,11},{10,... | collective-permute-start | bytes 1130504 | tf_op jit(solution)/shard_map/ppermute | solution.py:104
  10.4 13.8 %collective-permute-done.12 = bf16[736,256]{1,0:T(8,128)(2,1)S(1)} collective-permute-done((bf16[736,256]{1,0:T(8,128)(2,1)S(1)}, bf16[736,256]{1,0:T(8,128)(2,1)S(1)}, u32[]{:S(2)}, u32[]{:S(2)}) %collective-permute-start.12) | collective-permute-done | bytes 376864 | tf_op jit(solution)/shard_map/ppermute | solution.py:104
  24.2 1.6 %collective-permute-start.14 = (bf16[736,256]{1,0:T(8,128)(2,1)S(1)}, bf16[736,256]{1,0:T(8,128)(2,1)S(1)}, u32[]{:S(2)}, u32[]{:S(2)}) collective-permute-start(bf16[736,256]{1,0:T(8,128)(2,1)S(1)} %collective-permute-done.12), channel_id=1, source_target_pairs={{0,2},{1,3},{2,0},{3,1},{4,6},{5,7},{6,4},{7,5},{8,10},{9,11},{10,... | collective-permute-start | bytes 1130504 | tf_op jit(solution)/shard_map/ppermute | solution.py:104
  25.9 0.6 collective-permute-start.18
  26.5 0.3 collective-permute-start.2
  26.9 0.6 collective-permute-start.7
  27.5 0.8 collective-permute-done.2
  28.3 0.2 collective-permute-start.6
  28.6 0.1 pad_maximum_fusion.3
  28.7 0.1 pad_maximum_fusion.1
  28.8 0.1 dynamic-slice_bitcast_fusion.27
  28.9 1.1 %copy-done.3 = bf16[1,1440,360]{2,1,0:T(8,128)(2,1)S(1)} copy-done((bf16[1,1440,360]{2,1,0:T(8,128)(2,1)S(1)}, bf16[1,1440,360]{2,1,0:T(8,128)(2,1)}, u32[]{:S(2)}) %copy-start.3) | copy-done | bytes 1036824
  30.0 0.6 convolution_bitcast_fusion.6
  30.6 0.5 fusion.16
  31.1 0.8 copy-done.4
  31.9 0.7 multiply_convert_fusion.3
  32.5 0.8 convolution_convert_fusion.5
  33.4 2.6 %collective-permute-done.14 = bf16[736,256]{1,0:T(8,128)(2,1)S(1)} collective-permute-done((bf16[736,256]{1,0:T(8,128)(2,1)S(1)}, bf16[736,256]{1,0:T(8,128)(2,1)S(1)}, u32[]{:S(2)}, u32[]{:S(2)}) %collective-permute-start.14) | collective-permute-done | bytes 376864 | tf_op jit(solution)/shard_map/ppermute | solution.py:104
  36.0 1.1 %collective-permute-done.18 = bf16[736,256]{1,0:T(8,128)(2,1)S(1)} collective-permute-done((bf16[736,256]{1,0:T(8,128)(2,1)S(1)}, bf16[736,256]{1,0:T(8,128)(2,1)S(1)}, u32[]{:S(2)}, u32[]{:S(2)}) %collective-permute-start.18) | collective-permute-done | bytes 376864 | tf_op jit(solution)/shard_map/ppermute | solution.py:104
  37.1 5.1 %collective-permute-done.7 = bf16[736,256]{1,0:T(8,128)(2,1)S(1)} collective-permute-done((bf16[736,256]{1,0:T(8,128)(2,1)S(1)}, bf16[736,256]{1,0:T(8,128)(2,1)S(1)}, u32[]{:S(2)}, u32[]{:S(2)}) %collective-permute-start.7) | collective-permute-done | bytes 376864 | tf_op jit(solution)/shard_map/ppermute | solution.py:104
  42.3 1.2 %collective-permute-start.20 = (bf16[736,256]{1,0:T(8,128)(2,1)S(1)}, bf16[736,256]{1,0:T(8,128)(2,1)S(1)}, u32[]{:S(2)}, u32[]{:S(2)}) collective-permute-start(bf16[736,256]{1,0:T(8,128)(2,1)S(1)} %collective-permute-done.18), channel_id=1, source_target_pairs={{0,2},{1,3},{2,0},{3,1},{4,6},{5,7},{6,4},{7,5},{8,10},{9,11},{10,... | collective-permute-start | bytes 1130504 | tf_op jit(solution)/shard_map/ppermute | solution.py:104
  43.8 0.6 collective-permute-start.8
  44.5 0.8 collective-permute-start.4
  45.4 0.1 pad_maximum_fusion.11
  45.5 0.1 pad_maximum_fusion.9
  45.6 0.1 dynamic-slice_bitcast_fusion.11
  45.7 0.5 fusion.19
  46.3 0.6 convolution_bitcast_fusion.2
  47.2 0.1 dynamic-slice_bitcast_fusion.19
  47.3 0.5 fusion.21
  47.9 0.6 convolution_bitcast_fusion.4
  48.5 0.7 multiply_convert_fusion.1
  49.2 0.8 convolution_convert_fusion.3
  50.2 0.7 multiply_convert_fusion.2
  50.8 0.8 convolution_convert_fusion.4
  51.7 0.6 collective-permute-start.9
  52.3 0.9 %collective-permute-done.20 = bf16[736,256]{1,0:T(8,128)(2,1)S(1)} collective-permute-done((bf16[736,256]{1,0:T(8,128)(2,1)S(1)}, bf16[736,256]{1,0:T(8,128)(2,1)S(1)}, u32[]{:S(2)}, u32[]{:S(2)}) %collective-permute-start.20) | collective-permute-done | bytes 376864 | tf_op jit(solution)/shard_map/ppermute | solution.py:104
  53.5 1.0 %collective-permute-start.17 = (bf16[360,256]{1,0:T(8,128)(2,1)S(1)}, bf16[360,256]{1,0:T(8,128)(2,1)S(1)}, u32[]{:S(2)}, u32[]{:S(2)}) collective-permute-start(bf16[360,256]{1,0:T(8,128)(2,1)S(1)} %fusion.60), channel_id=1, source_target_pairs={{0,2},{1,3},{2,0},{3,1},{4,6},{5,7},{6,4},{7,5},{8,10},{9,11},{10,... | collective-permute-start | bytes 552968 | tf_op jit(solution)/shard_map/ppermute | solution.py:104
  54.6 1.1 %collective-permute-start.10 = (bf16[360,256]{1,0:T(8,128)(2,1)S(1)}, bf16[360,256]{1,0:T(8,128)(2,1)S(1)}, u32[]{:S(2)}, u32[]{:S(2)}) collective-permute-start(bf16[360,256]{1,0:T(8,128)(2,1)S(1)} %fusion.58), channel_id=1, source_target_pairs={{0,2},{1,3},{2,0},{3,1},{4,6},{5,7},{6,4},{7,5},{8,10},{9,11},{10,... | collective-permute-start | bytes 552968 | tf_op jit(solution)/shard_map/ppermute | solution.py:104
  55.7 0.2 pad_maximum_fusion.13
  56.0 0.5 fusion.17
  56.6 0.8 convolution_bitcast_fusion
  57.5 0.7 multiply_convert_fusion
  58.2 0.8 convolution_convert_fusion.2
  59.2 0.1 constant_dynamic-update-slice_fusion.3
  59.4 0.1 constant_dynamic-update-slice_fusion.2
  59.6 0.1 constant_dynamic-update-slice_fusion.1
  59.7 0.1 constant_dynamic-update-slice_fusion
  59.8 2.4 %fusion.13 = bf16[1,360,1440]{2,1,0:T(8,128)(2,1)} fusion(bf16[1440,256]{1,0:T(8,128)(2,1)S(1)} %pad_maximum_fusion.14, bf16[1440,256]{1,0:T(8,128)(2,1)S(1)} %pad_maximum_fusion.10, bf16[1440,256]{1,0:T(8,128)(2,1)S(1)} %pad_maximum_fusion.6, bf16[1440,256]{1,0:T(8,128)(2,1)S(1)} %pad_maximum_fusion.2, bf16[360,256]{1,0:T(8,128)(2,1)S(1)} %get-tuple-element.43, ...), kind=kOutput, calls=%fused_computation.17 | convolution fusion | flops 1076947200 | bytes 4723200 | tf_op jit(solution)/shard_map/dot_general | solution.py:181
  62.2 1.0 %collective-permute-start.23 = (bf16[360,256]{1,0:T(8,128)(2,1)S(1)}, bf16[360,256]{1,0:T(8,128)(2,1)S(1)}, u32[]{:S(2)}, u32[]{:S(2)}) collective-permute-start(bf16[360,256]{1,0:T(8,128)(2,1)S(1)} %fusion.62), channel_id=1, source_target_pairs={{0,2},{1,3},{2,0},{3,1},{4,6},{5,7},{6,4},{7,5},{8,10},{9,11},{10,... | collective-permute-start | bytes 552968 | tf_op jit(solution)/shard_map/ppermute | solution.py:104
  63.2 2.7 %fusion.12 = bf16[1,1440,360]{2,1,0:T(8,128)(2,1)} fusion(bf16[1440,1024]{1,0:T(8,128)(2,1)S(1)} %constant_dynamic-update-slice_fusion, bf16[720,1024]{1,0:T(8,128)(2,1)S(1)} %constant_dynamic-update-slice_fusion.4), kind=kOutput, calls=%fused_computation.12 | convolution fusion | flops 1062201600 | bytes 4723200 | tf_op jit(solution)/shard_map/dot_general | solution.py:180
  65.9 3.4 %collective-permute-done.23 = bf16[360,256]{1,0:T(8,128)(2,1)S(1)} collective-permute-done((bf16[360,256]{1,0:T(8,128)(2,1)S(1)}, bf16[360,256]{1,0:T(8,128)(2,1)S(1)}, u32[]{:S(2)}, u32[]{:S(2)}) %collective-permute-start.23) | collective-permute-done | bytes 184352 | tf_op jit(solution)/shard_map/ppermute | solution.py:104
  69.4 2.2 %collective-permute-start.24 = (bf16[360,256]{1,0:T(8,128)(2,1)S(1)}, bf16[360,256]{1,0:T(8,128)(2,1)S(1)}, u32[]{:S(2)}, u32[]{:S(2)}) collective-permute-start(bf16[360,256]{1,0:T(8,128)(2,1)S(1)} %fusion.35), channel_id=1, source_target_pairs={{0,4},{4,0},{8,12},{12,8},{1,5},{5,1},{9,13},{13,9},{2,6},{6,2},{1... | collective-permute-start | bytes 552968 | tf_op jit(solution)/shard_map/ppermute | solution.py:104
  71.8 5.3 %collective-permute-done.24 = bf16[360,256]{1,0:T(8,128)(2,1)S(1)} collective-permute-done((bf16[360,256]{1,0:T(8,128)(2,1)S(1)}, bf16[360,256]{1,0:T(8,128)(2,1)S(1)}, u32[]{:S(2)}, u32[]{:S(2)}) %collective-permute-start.24) | collective-permute-done | bytes 184352 | tf_op jit(solution)/shard_map/ppermute | solution.py:104
  77.1 0.1 add_convert_fusion.1
  77.2 3.4 %collective-permute-start.25 = (bf16[360,256]{1,0:T(8,128)(2,1)S(1)}, bf16[360,256]{1,0:T(8,128)(2,1)S(1)}, u32[]{:S(2)}, u32[]{:S(2)}) collective-permute-start(bf16[360,256]{1,0:T(8,128)(2,1)S(1)} %add_convert_fusion.1), channel_id=1, source_target_pairs={{0,8},{4,12},{8,0},{12,4},{1,9},{5,13},{9,1},{13,5},{2,10},{6,14},... | collective-permute-start | bytes 552968 | tf_op jit(solution)/shard_map/ppermute | solution.py:104
  80.7 2.7 %fusion.11 = bf16[1,1440,360]{2,1,0:T(8,128)(2,1)} fusion(bf16[1440,1024]{1,0:T(8,128)(2,1)S(1)} %constant_dynamic-update-slice_fusion, bf16[720,1024]{1,0:T(8,128)(2,1)S(1)} %constant_dynamic-update-slice_fusion.4), kind=kOutput, calls=%fused_computation.11 | convolution fusion | flops 1062201600 | bytes 4723200 | tf_op jit(solution)/shard_map/dot_general | solution.py:179
  83.4 4.6 %collective-permute-done.25 = bf16[360,256]{1,0:T(8,128)(2,1)S(1)} collective-permute-done((bf16[360,256]{1,0:T(8,128)(2,1)S(1)}, bf16[360,256]{1,0:T(8,128)(2,1)S(1)}, u32[]{:S(2)}, u32[]{:S(2)}) %collective-permute-start.25) | collective-permute-done | bytes 184352 | tf_op jit(solution)/shard_map/ppermute | solution.py:104
  88.0 0.8 fusion.63
  (87 shorter events, 2.6 us)
Async XLA Ops:
  0.6 30.0 %copy-start = (bf16[1,360,1440]{2,1,0:T(8,128)(2,1)S(1)}, bf16[1,360,1440]{2,1,0:T(8,128)(2,1)}, u32[]{:S(2)}) copy-start(bf16[1,360,1440]{2,1,0:T(8,128)(2,1)} %param.15) | copy-start | bytes 3110404
  3.2 21.0 %collective-permute-start.12 = (bf16[736,256]{1,0:T(8,128)(2,1)S(1)}, bf16[736,256]{1,0:T(8,128)(2,1)S(1)}, u32[]{:S(2)}, u32[]{:S(2)}) collective-permute-start(bf16[736,256]{1,0:T(8,128)(2,1)S(1)} %fusion.34), channel_id=1, source_target_pairs={{0,8},{4,12},{8,0},{12,4},{1,9},{5,13},{9,1},{13,5},{2,10},{6,14},... | collective-permute-start | bytes 1130504 | tf_op jit(solution)/shard_map/ppermute | solution.py:104
  7.3 19.3 %collective-permute-start.5 = (bf16[736,256]{1,0:T(8,128)(2,1)S(1)}, bf16[736,256]{1,0:T(8,128)(2,1)S(1)}, u32[]{:S(2)}, u32[]{:S(2)}) collective-permute-start(bf16[736,256]{1,0:T(8,128)(2,1)S(1)} %fusion.34), channel_id=1, source_target_pairs={{0,4},{4,0},{8,12},{12,8},{1,5},{5,1},{9,13},{13,9},{2,6},{6,2},{1... | collective-permute-start | bytes 1130504 | tf_op jit(solution)/shard_map/ppermute | solution.py:104
  8.8 17.0 %collective-permute-start.1 = (bf16[736,256]{1,0:T(8,128)(2,1)S(1)}, bf16[736,256]{1,0:T(8,128)(2,1)S(1)}, u32[]{:S(2)}, u32[]{:S(2)}) collective-permute-start(bf16[736,256]{1,0:T(8,128)(2,1)S(1)} %fusion.34), channel_id=1, source_target_pairs={{0,2},{1,3},{2,0},{3,1},{4,6},{5,7},{6,4},{7,5},{8,10},{9,11},{10,... | collective-permute-start | bytes 1130504 | tf_op jit(solution)/shard_map/ppermute | solution.py:104
  10.3 16.6 %collective-permute-start = (bf16[736,256]{1,0:T(8,128)(2,1)S(1)}, bf16[736,256]{1,0:T(8,128)(2,1)S(1)}, u32[]{:S(2)}, u32[]{:S(2)}) collective-permute-start(bf16[736,256]{1,0:T(8,128)(2,1)S(1)} %fusion.34), channel_id=1, source_target_pairs={{0,1},{1,0},{2,3},{3,2},{4,5},{5,4},{6,7},{7,6},{8,9},{9,8},{10,11... | collective-permute-start | bytes 1130504 | tf_op jit(solution)/shard_map/ppermute | solution.py:104
  24.2 11.8 %collective-permute-start.14 = (bf16[736,256]{1,0:T(8,128)(2,1)S(1)}, bf16[736,256]{1,0:T(8,128)(2,1)S(1)}, u32[]{:S(2)}, u32[]{:S(2)}) collective-permute-start(bf16[736,256]{1,0:T(8,128)(2,1)S(1)} %collective-permute-done.12), channel_id=1, source_target_pairs={{0,2},{1,3},{2,0},{3,1},{4,6},{5,7},{6,4},{7,5},{8,10},{9,11},{10,... | collective-permute-start | bytes 1130504 | tf_op jit(solution)/shard_map/ppermute | solution.py:104
  25.8 18.0 %collective-permute-start.13 = (bf16[736,256]{1,0:T(8,128)(2,1)S(1)}, bf16[736,256]{1,0:T(8,128)(2,1)S(1)}, u32[]{:S(2)}, u32[]{:S(2)}) collective-permute-start(bf16[736,256]{1,0:T(8,128)(2,1)S(1)} %collective-permute-done.12), channel_id=1, source_target_pairs={{0,1},{1,0},{2,3},{3,2},{4,5},{5,4},{6,7},{7,6},{8,9},{9,8},{10,11... | collective-permute-start | bytes 1130504 | tf_op jit(solution)/shard_map/ppermute | solution.py:104
  25.8 2.7 %copy-start.1 = (bf16[256,360]{0,1:T(8,128)(2,1)S(1)}, bf16[256,360]{0,1:T(8,128)(2,1)}, u32[]{:S(2)}) copy-start(bf16[256,360]{0,1:T(8,128)(2,1)} %param.9) | copy-start | bytes 552964
  25.9 11.2 %collective-permute-start.18 = (bf16[736,256]{1,0:T(8,128)(2,1)S(1)}, bf16[736,256]{1,0:T(8,128)(2,1)S(1)}, u32[]{:S(2)}, u32[]{:S(2)}) collective-permute-start(bf16[736,256]{1,0:T(8,128)(2,1)S(1)} %collective-permute-done.12), channel_id=1, source_target_pairs={{0,4},{4,0},{8,12},{12,8},{1,5},{5,1},{9,13},{13,9},{2,6},{6,2},{1... | collective-permute-start | bytes 1130504 | tf_op jit(solution)/shard_map/ppermute | solution.py:104
  26.5 1.8 %collective-permute-start.2 = (bf16[736,256]{1,0:T(8,128)(2,1)S(1)}, bf16[736,256]{1,0:T(8,128)(2,1)S(1)}, u32[]{:S(2)}, u32[]{:S(2)}) collective-permute-start(bf16[736,256]{1,0:T(8,128)(2,1)S(1)} %collective-permute-done.1), channel_id=1, source_target_pairs={{0,1},{1,0},{2,3},{3,2},{4,5},{5,4},{6,7},{7,6},{8,9},{9,8},{10,11... | collective-permute-start | bytes 1130504 | tf_op jit(solution)/shard_map/ppermute | solution.py:104
  26.9 1.8 %copy-start.2 = (bf16[256,360]{0,1:T(8,128)(2,1)S(1)}, bf16[256,360]{0,1:T(8,128)(2,1)}, u32[]{:S(2)}) copy-start(bf16[256,360]{0,1:T(8,128)(2,1)} %param.10) | copy-start | bytes 552964
  26.9 15.4 %collective-permute-start.7 = (bf16[736,256]{1,0:T(8,128)(2,1)S(1)}, bf16[736,256]{1,0:T(8,128)(2,1)S(1)}, u32[]{:S(2)}, u32[]{:S(2)}) collective-permute-start(bf16[736,256]{1,0:T(8,128)(2,1)S(1)} %collective-permute-done.5), channel_id=1, source_target_pairs={{0,2},{1,3},{2,0},{3,1},{4,6},{5,7},{6,4},{7,5},{8,10},{9,11},{10,... | collective-permute-start | bytes 1130504 | tf_op jit(solution)/shard_map/ppermute | solution.py:104
  28.3 15.3 %collective-permute-start.6 = (bf16[736,256]{1,0:T(8,128)(2,1)S(1)}, bf16[736,256]{1,0:T(8,128)(2,1)S(1)}, u32[]{:S(2)}, u32[]{:S(2)}) collective-permute-start(bf16[736,256]{1,0:T(8,128)(2,1)S(1)} %collective-permute-done.5), channel_id=1, source_target_pairs={{0,1},{1,0},{2,3},{3,2},{4,5},{5,4},{6,7},{7,6},{8,9},{9,8},{10,11... | collective-permute-start | bytes 1130504 | tf_op jit(solution)/shard_map/ppermute | solution.py:104
  28.8 1.2 %copy-start.3 = (bf16[1,1440,360]{2,1,0:T(8,128)(2,1)S(1)}, bf16[1,1440,360]{2,1,0:T(8,128)(2,1)}, u32[]{:S(2)}) copy-start(bf16[1,1440,360]{2,1,0:T(8,128)(2,1)} %param.13) | copy-start | bytes 3110404
  30.6 1.2 %copy-start.4 = (bf16[1,1440,360]{2,1,0:T(8,128)(2,1)S(1)}, bf16[1,1440,360]{2,1,0:T(8,128)(2,1)}, u32[]{:S(2)}) copy-start(bf16[1,1440,360]{2,1,0:T(8,128)(2,1)} %param.14) | copy-start | bytes 3110404
  36.0 8.4 %collective-permute-start.3 = (bf16[2,360,256]{2,1,0:T(8,128)(2,1)S(1)}, bf16[2,360,256]{2,1,0:T(8,128)(2,1)S(1)}, u32[]{:S(2)}, u32[]{:S(2)}) collective-permute-start(bf16[2,360,256]{2,1,0:T(8,128)(2,1)S(1)} %pad_maximum_fusion.18), channel_id=1, source_target_pairs={{0,1},{1,0},{2,3},{3,2},{4,5},{5,4},{6,7},{7,6},{8,9},{9,8},{10,11... | collective-permute-start | bytes 1105928 | tf_op jit(solution)/shard_map/ppermute | solution.py:104
  37.1 8.3 %collective-permute-start.15 = (bf16[736,256]{1,0:T(8,128)(2,1)S(1)}, bf16[736,256]{1,0:T(8,128)(2,1)S(1)}, u32[]{:S(2)}, u32[]{:S(2)}) collective-permute-start(bf16[736,256]{1,0:T(8,128)(2,1)S(1)} %collective-permute-done.14), channel_id=1, source_target_pairs={{0,1},{1,0},{2,3},{3,2},{4,5},{5,4},{6,7},{7,6},{8,9},{9,8},{10,11... | collective-permute-start | bytes 1130504 | tf_op jit(solution)/shard_map/ppermute | solution.py:104
  42.3 10.9 %collective-permute-start.20 = (bf16[736,256]{1,0:T(8,128)(2,1)S(1)}, bf16[736,256]{1,0:T(8,128)(2,1)S(1)}, u32[]{:S(2)}, u32[]{:S(2)}) collective-permute-start(bf16[736,256]{1,0:T(8,128)(2,1)S(1)} %collective-permute-done.18), channel_id=1, source_target_pairs={{0,2},{1,3},{2,0},{3,1},{4,6},{5,7},{6,4},{7,5},{8,10},{9,11},{10,... | collective-permute-start | bytes 1130504 | tf_op jit(solution)/shard_map/ppermute | solution.py:104
  43.6 9.7 %collective-permute-start.19 = (bf16[736,256]{1,0:T(8,128)(2,1)S(1)}, bf16[736,256]{1,0:T(8,128)(2,1)S(1)}, u32[]{:S(2)}, u32[]{:S(2)}) collective-permute-start(bf16[736,256]{1,0:T(8,128)(2,1)S(1)} %collective-permute-done.18), channel_id=1, source_target_pairs={{0,1},{1,0},{2,3},{3,2},{4,5},{5,4},{6,7},{7,6},{8,9},{9,8},{10,11... | collective-permute-start | bytes 1130504 | tf_op jit(solution)/shard_map/ppermute | solution.py:104
  43.8 3.1 %collective-permute-start.8 = (bf16[736,256]{1,0:T(8,128)(2,1)S(1)}, bf16[736,256]{1,0:T(8,128)(2,1)S(1)}, u32[]{:S(2)}, u32[]{:S(2)}) collective-permute-start(bf16[736,256]{1,0:T(8,128)(2,1)S(1)} %collective-permute-done.7), channel_id=1, source_target_pairs={{0,1},{1,0},{2,3},{3,2},{4,5},{5,4},{6,7},{7,6},{8,9},{9,8},{10,11... | collective-permute-start | bytes 1130504 | tf_op jit(solution)/shard_map/ppermute | solution.py:104
  44.5 38.9 %collective-permute-start.4 = (bf16[360,256]{1,0:T(8,128)(2,1)S(1)}, bf16[360,256]{1,0:T(8,128)(2,1)S(1)}, u32[]{:S(2)}, u32[]{:S(2)}) collective-permute-start(bf16[360,256]{1,0:T(8,128)(2,1)S(1)} %fusion.56), channel_id=1, source_target_pairs={{0,2},{1,3},{2,0},{3,1},{4,6},{5,7},{6,4},{7,5},{8,10},{9,11},{10,... | collective-permute-start | bytes 552968 | tf_op jit(solution)/shard_map/ppermute | solution.py:104
  50.1 3.3 %collective-permute-start.16 = (bf16[2,360,256]{2,1,0:T(8,128)(2,1)S(1)}, bf16[2,360,256]{2,1,0:T(8,128)(2,1)S(1)}, u32[]{:S(2)}, u32[]{:S(2)}) collective-permute-start(bf16[2,360,256]{2,1,0:T(8,128)(2,1)S(1)} %pad_maximum_fusion.22), channel_id=1, source_target_pairs={{0,1},{1,0},{2,3},{3,2},{4,5},{5,4},{6,7},{7,6},{8,9},{9,8},{10,11... | collective-permute-start | bytes 1105928 | tf_op jit(solution)/shard_map/ppermute | solution.py:104
  51.7 2.8 %collective-permute-start.9 = (bf16[2,360,256]{2,1,0:T(8,128)(2,1)S(1)}, bf16[2,360,256]{2,1,0:T(8,128)(2,1)S(1)}, u32[]{:S(2)}, u32[]{:S(2)}) collective-permute-start(bf16[2,360,256]{2,1,0:T(8,128)(2,1)S(1)} %pad_maximum_fusion.20), channel_id=1, source_target_pairs={{0,1},{1,0},{2,3},{3,2},{4,5},{5,4},{6,7},{7,6},{8,9},{9,8},{10,11... | collective-permute-start | bytes 1105928 | tf_op jit(solution)/shard_map/ppermute | solution.py:104
  53.2 2.5 %collective-permute-start.21 = (bf16[736,256]{1,0:T(8,128)(2,1)S(1)}, bf16[736,256]{1,0:T(8,128)(2,1)S(1)}, u32[]{:S(2)}, u32[]{:S(2)}) collective-permute-start(bf16[736,256]{1,0:T(8,128)(2,1)S(1)} %collective-permute-done.20), channel_id=1, source_target_pairs={{0,1},{1,0},{2,3},{3,2},{4,5},{5,4},{6,7},{7,6},{8,9},{9,8},{10,11... | collective-permute-start | bytes 1130504 | tf_op jit(solution)/shard_map/ppermute | solution.py:104
  53.5 18.3 %collective-permute-start.17 = (bf16[360,256]{1,0:T(8,128)(2,1)S(1)}, bf16[360,256]{1,0:T(8,128)(2,1)S(1)}, u32[]{:S(2)}, u32[]{:S(2)}) collective-permute-start(bf16[360,256]{1,0:T(8,128)(2,1)S(1)} %fusion.60), channel_id=1, source_target_pairs={{0,2},{1,3},{2,0},{3,1},{4,6},{5,7},{6,4},{7,5},{8,10},{9,11},{10,... | collective-permute-start | bytes 552968 | tf_op jit(solution)/shard_map/ppermute | solution.py:104
  54.6 17.1 %collective-permute-start.10 = (bf16[360,256]{1,0:T(8,128)(2,1)S(1)}, bf16[360,256]{1,0:T(8,128)(2,1)S(1)}, u32[]{:S(2)}, u32[]{:S(2)}) collective-permute-start(bf16[360,256]{1,0:T(8,128)(2,1)S(1)} %fusion.58), channel_id=1, source_target_pairs={{0,2},{1,3},{2,0},{3,1},{4,6},{5,7},{6,4},{7,5},{8,10},{9,11},{10,... | collective-permute-start | bytes 552968 | tf_op jit(solution)/shard_map/ppermute | solution.py:104
  59.1 3.1 %collective-permute-start.22 = (bf16[2,360,256]{2,1,0:T(8,128)(2,1)S(1)}, bf16[2,360,256]{2,1,0:T(8,128)(2,1)S(1)}, u32[]{:S(2)}, u32[]{:S(2)}) collective-permute-start(bf16[2,360,256]{2,1,0:T(8,128)(2,1)S(1)} %pad_maximum_fusion.24), channel_id=1, source_target_pairs={{0,1},{1,0},{2,3},{3,2},{4,5},{5,4},{6,7},{7,6},{8,9},{9,8},{10,11... | collective-permute-start | bytes 1105928 | tf_op jit(solution)/shard_map/ppermute | solution.py:104
  62.2 7.1 %collective-permute-start.23 = (bf16[360,256]{1,0:T(8,128)(2,1)S(1)}, bf16[360,256]{1,0:T(8,128)(2,1)S(1)}, u32[]{:S(2)}, u32[]{:S(2)}) collective-permute-start(bf16[360,256]{1,0:T(8,128)(2,1)S(1)} %fusion.62), channel_id=1, source_target_pairs={{0,2},{1,3},{2,0},{3,1},{4,6},{5,7},{6,4},{7,5},{8,10},{9,11},{10,... | collective-permute-start | bytes 552968 | tf_op jit(solution)/shard_map/ppermute | solution.py:104
  69.4 7.7 %collective-permute-start.24 = (bf16[360,256]{1,0:T(8,128)(2,1)S(1)}, bf16[360,256]{1,0:T(8,128)(2,1)S(1)}, u32[]{:S(2)}, u32[]{:S(2)}) collective-permute-start(bf16[360,256]{1,0:T(8,128)(2,1)S(1)} %fusion.35), channel_id=1, source_target_pairs={{0,4},{4,0},{8,12},{12,8},{1,5},{5,1},{9,13},{13,9},{2,6},{6,2},{1... | collective-permute-start | bytes 552968 | tf_op jit(solution)/shard_map/ppermute | solution.py:104
  71.7 11.7 %collective-permute-start.11 = (bf16[360,256]{1,0:T(8,128)(2,1)S(1)}, bf16[360,256]{1,0:T(8,128)(2,1)S(1)}, u32[]{:S(2)}, u32[]{:S(2)}) collective-permute-start(bf16[360,256]{1,0:T(8,128)(2,1)S(1)} %fusion.37), channel_id=1, source_target_pairs={{0,4},{4,0},{8,12},{12,8},{1,5},{5,1},{9,13},{13,9},{2,6},{6,2},{1... | collective-permute-start | bytes 552968 | tf_op jit(solution)/shard_map/ppermute | solution.py:104
  77.2 10.8 %collective-permute-start.25 = (bf16[360,256]{1,0:T(8,128)(2,1)S(1)}, bf16[360,256]{1,0:T(8,128)(2,1)S(1)}, u32[]{:S(2)}, u32[]{:S(2)}) collective-permute-start(bf16[360,256]{1,0:T(8,128)(2,1)S(1)} %add_convert_fusion.1), channel_id=1, source_target_pairs={{0,8},{4,12},{8,0},{12,4},{1,9},{5,13},{9,1},{13,5},{2,10},{6,14},... | collective-permute-start | bytes 552968 | tf_op jit(solution)/shard_map/ppermute | solution.py:104

commit v2 on v1

--- a/solution.py
+++ b/solution.py
@@ -115,6 +115,14 @@
     return (a.astype(F32) + b.astype(F32)).astype(BF16)
 
 
+def after(value, *others):
+    head = value[:16].astype(F32)
+    for other in others:
+        zero = other[:16, :1].astype(F32)
+        head = head + jnp.where(zero > 3e38, zero, 0.0)
+    return lax.dynamic_update_slice(value, head.astype(value.dtype), (0,) * value.ndim)
+
+
 def per_device(tokens, out_grad, routes, route_probs, w_gate, w_up, w_down):
     experts, partners = lax.axis_size("expert"), lax.axis_size("tensor")
     token_count, route_count = routes.shape
@@ -124,30 +132,23 @@
     me = lax.axis_index("tensor")
     here = lax.axis_index("expert")
 
-    named = routes[:, :, None] == jnp.arange(experts, dtype=jnp.int32)[None, None, :]
-    by_expert = jnp.sum(jnp.where(named, route_probs.astype(F32)[:, :, None], 0.0), axis=1)
-    weights = jnp.zeros((16, token_count), BF16).at[:experts].set(by_expert.T.astype(BF16))
+    ids, probs = routes.T[:, None, :], route_probs.T[:, None, :]
+    expert = lax.broadcasted_iota(jnp.int32, (route_count, 16, token_count), 1)
+    weights = jnp.sum(jnp.where(ids == expert, probs, jnp.zeros((), BF16)), axis=0)
     own = jnp.concatenate([tokens.T, out_grad.T, weights])
 
-    z1 = swap(own, "expert", 1)
-    z2 = swap(own, "expert", 2)
-    z3 = swap(z2, "expert", 1)
-
-    gate_t = w_gate[0].T
-    up_t = w_up[0].T
-    down = w_down[0]
-    both = jnp.concatenate([w_gate[0], w_up[0]], axis=1)
-
-    def forward(block):
-        far = swap(block, "tensor", 2)
-        near = swap(block, "tensor", 1)
-        diagonal = swap(far, "tensor", 1)
+    gate, up, down = w_gate[0], w_up[0], w_down[0]
+    both = jnp.concatenate([gate, up], axis=1)
+    first = (((0,), (0,)), ((), ()))
+    lanes = (((1,), (1,)), ((), ()))
+
+    def forward(block, near, far, diagonal):
         pieces = (block, near, far, diagonal)
         x = in_order([p[:width] for p in pieces], me)
         dy = in_order([p[width : 2 * width] for p in pieces], me)
         weight = lax.dynamic_slice_in_dim(block, 2 * width + here, 1, 0).astype(F32)
-        pre_gate = jnp.dot(gate_t, x, preferred_element_type=F32)
-        pre_up = jnp.dot(up_t, x, preferred_element_type=F32)
+        pre_gate = lax.dot_general(gate, x, first, preferred_element_type=F32)
+        pre_up = lax.dot_general(up, x, first, preferred_element_type=F32)
         hidden_grad = jnp.dot(down, dy, preferred_element_type=F32) * weight
         sigmoid_gate = jax.nn.sigmoid(pre_gate)
         activated = pre_gate * sigmoid_gate
@@ -160,25 +161,67 @@
         partial = jnp.dot(both, grads, preferred_element_type=F32).astype(BF16)
         partial = partial.reshape(partners, width, token_count)
         mine = [lax.dynamic_index_in_dim(partial, me ^ k, 0, keepdims=False) for k in range(4)]
-        got = swap(jnp.stack([mine[1], mine[3]]), "tensor", 1)
-        kept = add(mine[0], got[0])
-        sent = add(mine[2], got[1])
-        summed = add(kept, swap(sent, "tensor", 2))
-        return x, dy, grads, scaled_hidden, summed
-
-    parts = [forward(b) for b in (own, z1, z2, z3)]
-    s0, s1, s2, s3 = [p[4] for p in parts]
-    t0 = s0.astype(F32) + swap(s1, "expert", 1).astype(F32)
-    t2 = add(s2, swap(s3, "expert", 1))
-    grad_tokens = (t0 + swap(t2, "expert", 2).astype(F32)).astype(BF16).T
-
-    parts = lax.optimization_barrier([p[:4] for p in parts])
-    x, dy, grads, scaled = [jnp.concatenate([p[i] for p in parts], axis=1) for i in range(4)]
-    lanes = (((1,), (1,)), ((), ()))
-    half = grads.shape[0] // 2
-    grad_gate = lax.dot_general(x, grads[:half], lanes, preferred_element_type=F32).astype(BF16)
-    grad_up = lax.dot_general(x, grads[half:], lanes, preferred_element_type=F32).astype(BF16)
+        return (x, dy, grads, scaled_hidden), jnp.stack([mine[0], mine[2]]), jnp.stack([mine[1], mine[3]])
+
+    def over_core(kept, sent):
+        got = swap(sent, "tensor", 1)
+        return add(kept[0], got[0]), add(kept[1], got[1])
+
+    z2 = swap(own, "expert", 2)
+    z1 = swap(own, "expert", 1)
+    far0 = swap(own, "tensor", 2)
+    near0 = swap(own, "tensor", 1)
+    far2 = swap(z2, "tensor", 2)
+    z3 = swap(z2, "expert", 1)
+    near2 = swap(z2, "tensor", 1)
+    far0 = after(far0, z2)
+    diagonal0 = swap(far0, "tensor", 1)
+    data0, kept0, sent0 = forward(own, near0, far0, diagonal0)
+    far2 = after(far2, sent0[0])
+    far3 = swap(far2, "expert", 1)
+    diagonal2 = swap(far2, "tensor", 1)
+    z1 = after(z1, far2)
+    far1 = swap(z1, "tensor", 2)
+    near1 = swap(z1, "tensor", 1)
+    data2, kept2, sent2 = forward(z2, near2, far2, after(diagonal2, z1))
+    kept0, sent0 = over_core(kept0, jnp.stack([after(sent0[0], sent2[0]), sent0[1]]))
+    kept2, sent2 = over_core(kept2, sent2)
+    got2 = swap(sent2, "tensor", 2)
+    sent0 = after(sent0, sent2)
+    got0 = swap(sent0, "tensor", 2)
+    z3 = after(z3, sent2)
+    near3 = swap(z3, "tensor", 1)
+    far1 = after(far1, sent0)
+    diagonal1 = swap(far1, "tensor", 1)
+    far3 = after(far3, far1)
+    diagonal3 = swap(far3, "tensor", 1)
+    data1, kept1, sent1 = forward(z1, near1, far1, after(diagonal1, far3))
+    kept1, sent1 = over_core(kept1, sent1)
+    got1 = swap(sent1, "tensor", 2)
+    data3, kept3, sent3 = forward(z3, near3, after(far3, data1[3]), diagonal3)
+    kept3, sent3 = over_core(kept3, sent3)
+    got3 = swap(sent3, "tensor", 2)
+    sum2 = add(kept2, after(got2, sent3))
+    back2 = swap(sum2, "expert", 2)
+    sum1 = add(kept1, after(got1, sum2))
+    back1 = swap(sum1, "expert", 1)
+    sum3 = add(kept3, after(got3, sum1))
+    back3 = swap(sum3, "expert", 3)
+    got0 = after(got0, sum3)
+
+    parts = lax.optimization_barrier((data0, data1, data2, data3))
+
+    def joined(i):
+        return jnp.concatenate([p[i] for p in parts], axis=1)
+
+    x, dy = joined(0), joined(1)
+    grads, scaled = after(joined(2), sum2), after(joined(3), sum3)
+    ups = after(grads[width:], sum3)
+    grad_gate = lax.dot_general(x, grads[:width], lanes, preferred_element_type=F32).astype(BF16)
+    grad_up = lax.dot_general(x, ups, lanes, preferred_element_type=F32).astype(BF16)
     grad_down = lax.dot_general(scaled, dy, lanes, preferred_element_type=F32).astype(BF16)
+    grad_tokens = add(kept0, got0).astype(F32)
+    grad_tokens = (grad_tokens + back1.astype(F32) + back2.astype(F32) + back3.astype(F32)).astype(BF16).T
     return (grad_tokens, grad_gate[None], grad_up[None], grad_down[None])
 
 

time: 89.1 us -> 82 us (0.920)
  waiting for transfers between devices: 37.6 us -> 25.8 us
  other arithmetic: 5.32 us -> 7.4 us
  starting transfers between devices: 22.9 us -> 24.9 us
    ppermute x26, waiting for transfers between devices: 37.6 us -> 25.8 us  [swap(): return lax.ppermute(block, axis, [(i, i ^ bit) for i in range(size)])]
    ppermute x26, starting transfers between devices: 22.9 us -> 24.9 us  [swap(): return lax.ppermute(block, axis, [(i, i ^ bit) for i in range(size)])]
    select_n x0 -> x14, other arithmetic: none -> 1.59 us  [after(): head = head + jnp.where(zero > 3e+38, zero, 0.0)]
    dynamic_update_slice x0 -> x16, other arithmetic: none -> 1.18 us  [after(): lax.dynamic_update_slice(value, head.astype(value.dtype), (0,) * value.ndim)]
    unnamed x16 -> x20, local copies, waits for them, and re-layouts: 2.29 us -> 2.37 us
  transfers between devices with their start and end apart: 26 -> 26, of which waited for: 9 -> 9; matrix products, arithmetic and copies ran while one was open for 24% -> 31% of each run, Pallas kernels for 0% -> 0%
where the time goes in v2:
time: 82 us; the launch traced here: 81.8 us
  waiting for transfers between devices  25.8 us (31%)
  starting transfers between devices  24.9 us (30%)
  matrix products  18.7 us (23%)
  other arithmetic  7.4 us (9%)
  local copies, waits for them, and re-layouts  3.58 us (4%)
  between operations  1.39 us (2%)
    ppermute x26, waiting for transfers between devices, swap(): return lax.ppermute(block, axis, [(i, i ^ bit) for i in range(size)])  25.8 us
    ppermute x26, starting transfers between devices, swap(): return lax.ppermute(block, axis, [(i, i ^ bit) for i in range(size)])  24.9 us
    dot_general x4, matrix products, forward(): partial = jnp.dot(both, grads, preferred_element_type=F32).astype(BF16)  3.21 us
    dot_general x1, matrix products, per_device(): lax.dot_general(scaled, dy, lanes, preferred_element_type=F32).astype(BF16)  2.97 us
    dot_general x1, matrix products, per_device(): lax.dot_general(x, grads[:width], lanes, preferred_element_type=F32)  2.73 us
    dot_general x1, matrix products, per_device(): lax.dot_general(x, ups, lanes, preferred_element_type=F32).astype(BF16)  2.73 us
    dot_general x4, matrix products, forward(): pre_up = lax.dot_general(up, x, first, preferred_element_type=F32)  2.65 us
    dot_general x4, matrix products, forward(): pre_gate = lax.dot_general(gate, x, first, preferred_element_type=F32)  2.52 us
  transfers between devices with their start and end apart: 26, of which 9 were waited for; matrix products, arithmetic and copies ran while one was open for 31% of the time, Pallas kernels for 0%

profile of v2, /device:TPU:0, one launch (start us, length us, event | category | flops | bytes accessed | tf_op | source)
XLA Modules:
  0.0 81.8 jit_solution(4290015647323245039)
XLA Ops:
  0.6 0.8 fusion.57
  1.4 1.0 %pad_maximum_fusion.17 = bf16[736,256]{1,0:T(8,128)(2,1)S(1)} fusion(bf16[16,256]{1,0:T(8,128)(2,1)S(1)} %fusion.57, bf16[360,256]{1,0:T(8,128)(2,1)} %bitcast.291, bf16[360,256]{1,0:T(8,128)(2,1)} %bitcast.293), kind=kLoop, calls=%fused_computation.53 | loop fusion | flops 1130496 | bytes 753664 | tf_op jit(solution)/shard_map/concatenate | solution.py:138
  2.5 4.1 %collective-permute-start.2 = (bf16[736,256]{1,0:T(8,128)(2,1)S(1)}, bf16[736,256]{1,0:T(8,128)(2,1)S(1)}, u32[]{:S(2)}, u32[]{:S(2)}) collective-permute-start(bf16[736,256]{1,0:T(8,128)(2,1)S(1)} %pad_maximum_fusion.17), channel_id=1, source_target_pairs={{0,8},{4,12},{8,0},{12,4},{1,9},{5,13},{9,1},{13,5},{2,10},{6,14},... | collective-permute-start | bytes 1130504 | tf_op jit(solution)/shard_map/ppermute | solution.py:104
  6.6 1.5 %collective-permute-start.1 = (bf16[736,256]{1,0:T(8,128)(2,1)S(1)}, bf16[736,256]{1,0:T(8,128)(2,1)S(1)}, u32[]{:S(2)}, u32[]{:S(2)}) collective-permute-start(bf16[736,256]{1,0:T(8,128)(2,1)S(1)} %pad_maximum_fusion.17), channel_id=1, source_target_pairs={{0,2},{1,3},{2,0},{3,1},{4,6},{5,7},{6,4},{7,5},{8,10},{9,11},{10,... | collective-permute-start | bytes 1130504 | tf_op jit(solution)/shard_map/ppermute | solution.py:104
  8.1 1.6 %collective-permute-start.7 = (bf16[736,256]{1,0:T(8,128)(2,1)S(1)}, bf16[736,256]{1,0:T(8,128)(2,1)S(1)}, u32[]{:S(2)}, u32[]{:S(2)}) collective-permute-start(bf16[736,256]{1,0:T(8,128)(2,1)S(1)} %pad_maximum_fusion.17), channel_id=1, source_target_pairs={{0,4},{4,0},{8,12},{12,8},{1,5},{5,1},{9,13},{13,9},{2,6},{6,2},{1... | collective-permute-start | bytes 1130504 | tf_op jit(solution)/shard_map/ppermute | solution.py:104
  9.7 13.9 %collective-permute-done.2 = bf16[736,256]{1,0:T(8,128)(2,1)S(1)} collective-permute-done((bf16[736,256]{1,0:T(8,128)(2,1)S(1)}, bf16[736,256]{1,0:T(8,128)(2,1)S(1)}, u32[]{:S(2)}, u32[]{:S(2)}) %collective-permute-start.2) | collective-permute-done | bytes 376864 | tf_op jit(solution)/shard_map/ppermute | solution.py:104
  23.5 0.1 fusion.59
  23.9 1.6 %collective-permute-start.5 = (bf16[736,256]{1,0:T(8,128)(2,1)S(1)}, bf16[736,256]{1,0:T(8,128)(2,1)S(1)}, u32[]{:S(2)}, u32[]{:S(2)}) collective-permute-start(bf16[736,256]{1,0:T(8,128)(2,1)S(1)} %collective-permute-done.2), channel_id=1, source_target_pairs={{0,2},{1,3},{2,0},{3,1},{4,6},{5,7},{6,4},{7,5},{8,10},{9,11},{10,... | collective-permute-start | bytes 1130504 | tf_op jit(solution)/shard_map/ppermute | solution.py:104
  25.5 0.2 collective-permute-start.4
  25.7 0.6 collective-permute-start.11
  26.4 0.2 pad_maximum_fusion.1
  26.8 1.1 %copy-done.3 = bf16[1,1440,360]{2,1,0:T(8,128)(2,1)S(1)} copy-done((bf16[1,1440,360]{2,1,0:T(8,128)(2,1)S(1)}, bf16[1,1440,360]{2,1,0:T(8,128)(2,1)}, u32[]{:S(2)}) %copy-start.3) | copy-done | bytes 1036824
  27.9 0.6 convolution_bitcast_fusion.6
  28.5 0.5 fusion.16
  29.0 0.8 copy-done.4
  29.7 0.7 multiply_convert_fusion.2
  30.4 0.8 convolution_convert_fusion.5
  31.2 0.1 fusion.60
  31.3 3.7 %collective-permute-done.5 = bf16[736,256]{1,0:T(8,128)(2,1)S(1)} collective-permute-done((bf16[736,256]{1,0:T(8,128)(2,1)S(1)}, bf16[736,256]{1,0:T(8,128)(2,1)S(1)}, u32[]{:S(2)}, u32[]{:S(2)}) %collective-permute-start.5) | collective-permute-done | bytes 376864 | tf_op jit(solution)/shard_map/ppermute | solution.py:104
  35.2 0.1 fusion.61
  35.5 1.6 %collective-permute-start.14 = (bf16[736,256]{1,0:T(8,128)(2,1)S(1)}, bf16[736,256]{1,0:T(8,128)(2,1)S(1)}, u32[]{:S(2)}, u32[]{:S(2)}) collective-permute-start(bf16[736,256]{1,0:T(8,128)(2,1)S(1)} %get-tuple-element.42), channel_id=1, source_target_pairs={{0,2},{1,3},{2,0},{3,1},{4,6},{5,7},{6,4},{7,5},{8,10},{9,11},{10,... | collective-permute-start | bytes 1130504 | tf_op jit(solution)/shard_map/ppermute | solution.py:104
  37.1 0.2 collective-permute-start.6
  37.4 0.6 collective-permute-start.13
  38.1 0.1 fusion.62
  38.3 0.6 collective-permute-done.6
  39.2 0.5 fusion.21
  39.9 0.6 convolution_bitcast_fusion.4
  40.5 0.7 multiply_convert_fusion.1
  41.1 0.8 convolution_convert_fusion.4
  42.0 0.1 fusion.63
  42.2 0.2 collective-permute-start.9
  42.6 0.4 collective-permute-start.8
  43.0 0.9 %collective-permute-done.9 = bf16[2,360,256]{2,1,0:T(8,128)(2,1)S(1)} collective-permute-done((bf16[2,360,256]{2,1,0:T(8,128)(2,1)S(1)}, bf16[2,360,256]{2,1,0:T(8,128)(2,1)S(1)}, u32[]{:S(2)}, u32[]{:S(2)}) %collective-permute-start.9) | collective-permute-done | bytes 368672 | tf_op jit(solution)/shard_map/ppermute | solution.py:104
  44.0 0.5 collective-permute-start.22
  44.7 0.1 fusion.64
  44.9 1.5 %collective-permute-start.10 = (bf16[360,256]{1,0:T(8,128)(2,1)S(1)}, bf16[360,256]{1,0:T(8,128)(2,1)S(1)}, u32[]{:S(2)}, u32[]{:S(2)}) collective-permute-start(bf16[360,256]{1,0:T(8,128)(2,1)S(1)} %get-tuple-element.36), channel_id=1, source_target_pairs={{0,2},{1,3},{2,0},{3,1},{4,6},{5,7},{6,4},{7,5},{8,10},{9,11},{10,... | collective-permute-start | bytes 552968 | tf_op jit(solution)/shard_map/ppermute | solution.py:104
  46.4 0.1 fusion.65
  46.7 0.4 collective-permute-start.16
  47.1 0.1 fusion.66
  47.3 1.2 %collective-permute-done.13 = bf16[736,256]{1,0:T(8,128)(2,1)S(1)} collective-permute-done((bf16[736,256]{1,0:T(8,128)(2,1)S(1)}, bf16[736,256]{1,0:T(8,128)(2,1)S(1)}, u32[]{:S(2)}, u32[]{:S(2)}) %collective-permute-start.13) | collective-permute-done | bytes 376864 | tf_op jit(solution)/shard_map/ppermute | solution.py:104
  48.6 0.1 fusion.67
  49.2 0.6 convolution_bitcast_fusion.3
  49.8 0.5 fusion.17
  50.2 0.7 fusion.31
  50.9 0.1 fusion.68
  51.2 0.8 convolution_convert_fusion.2
  52.3 0.5 fusion.19
  53.0 0.8 convolution_bitcast_fusion
  53.9 0.7 multiply_convert_fusion
  54.6 0.8 convolution_convert_fusion.3
  55.5 0.6 collective-permute-start.20
  56.9 1.0 %collective-permute-done.18 = bf16[2,360,256]{2,1,0:T(8,128)(2,1)S(1)} collective-permute-done((bf16[2,360,256]{2,1,0:T(8,128)(2,1)S(1)}, bf16[2,360,256]{2,1,0:T(8,128)(2,1)S(1)}, u32[]{:S(2)}, u32[]{:S(2)}) %collective-permute-start.18) | collective-permute-done | bytes 368672 | tf_op jit(solution)/shard_map/ppermute | solution.py:104
  57.9 1.6 %collective-permute-start.19 = (bf16[360,256]{1,0:T(8,128)(2,1)S(1)}, bf16[360,256]{1,0:T(8,128)(2,1)S(1)}, u32[]{:S(2)}, u32[]{:S(2)}) collective-permute-start(bf16[360,256]{1,0:T(8,128)(2,1)S(1)} %fusion.48), channel_id=1, source_target_pairs={{0,2},{1,3},{2,0},{3,1},{4,6},{5,7},{6,4},{7,5},{8,10},{9,11},{10,... | collective-permute-start | bytes 552968 | tf_op jit(solution)/shard_map/ppermute | solution.py:104
  59.9 1.8 %collective-permute-start.24 = (bf16[360,256]{1,0:T(8,128)(2,1)S(1)}, bf16[360,256]{1,0:T(8,128)(2,1)S(1)}, u32[]{:S(2)}, u32[]{:S(2)}) collective-permute-start(bf16[360,256]{1,0:T(8,128)(2,1)S(1)} %fusion.25), channel_id=1, source_target_pairs={{0,8},{4,12},{8,0},{12,4},{1,9},{5,13},{9,1},{13,5},{2,10},{6,14},... | collective-permute-start | bytes 552968 | tf_op jit(solution)/shard_map/ppermute | solution.py:104
  61.8 1.4 %collective-permute-start.21 = (bf16[360,256]{1,0:T(8,128)(2,1)S(1)}, bf16[360,256]{1,0:T(8,128)(2,1)S(1)}, u32[]{:S(2)}, u32[]{:S(2)}) collective-permute-start(bf16[360,256]{1,0:T(8,128)(2,1)S(1)} %fusion.50), channel_id=1, source_target_pairs={{0,2},{1,3},{2,0},{3,1},{4,6},{5,7},{6,4},{7,5},{8,10},{9,11},{10,... | collective-permute-start | bytes 552968 | tf_op jit(solution)/shard_map/ppermute | solution.py:104
  63.3 2.7 %fusion.11 = bf16[1,1440,360]{2,1,0:T(8,128)(2,1)} fusion(bf16[1440,1024]{1,0:T(8,128)(2,1)S(1)} %constant_dynamic-update-slice_fusion, bf16[720,1024]{1,0:T(8,128)(2,1)S(1)} %fusion.53), kind=kOutput, calls=%fused_computation.11 | convolution fusion | flops 1062201600 | bytes 4723200 | tf_op jit(solution)/shard_map/dot_general | solution.py:220
  66.1 2.8 %collective-permute-done.21 = bf16[360,256]{1,0:T(8,128)(2,1)S(1)} collective-permute-done((bf16[360,256]{1,0:T(8,128)(2,1)S(1)}, bf16[360,256]{1,0:T(8,128)(2,1)S(1)}, u32[]{:S(2)}, u32[]{:S(2)}) %collective-permute-start.21) | collective-permute-done | bytes 184352 | tf_op jit(solution)/shard_map/ppermute | solution.py:104
  69.0 1.4 %collective-permute-start.23 = (bf16[360,256]{1,0:T(8,128)(2,1)S(1)}, bf16[360,256]{1,0:T(8,128)(2,1)S(1)}, u32[]{:S(2)}, u32[]{:S(2)}) collective-permute-start(bf16[360,256]{1,0:T(8,128)(2,1)S(1)} %fusion.26), channel_id=1, source_target_pairs={{0,4},{4,0},{8,12},{12,8},{1,5},{5,1},{9,13},{13,9},{2,6},{6,2},{1... | collective-permute-start | bytes 552968 | tf_op jit(solution)/shard_map/ppermute | solution.py:104
  70.7 0.1 fusion.72
  70.9 2.6 %collective-permute-start.25 = (bf16[360,256]{1,0:T(8,128)(2,1)S(1)}, bf16[360,256]{1,0:T(8,128)(2,1)S(1)}, u32[]{:S(2)}, u32[]{:S(2)}) collective-permute-start(bf16[360,256]{1,0:T(8,128)(2,1)S(1)} %fusion.27), channel_id=1, source_target_pairs={{0,12},{4,8},{8,4},{12,0},{1,13},{5,9},{9,5},{13,1},{2,14},{6,10},... | collective-permute-start | bytes 552968 | tf_op jit(solution)/shard_map/ppermute | solution.py:104
  73.5 3.0 %fusion.13 = bf16[1,360,1440]{2,1,0:T(8,128)(2,1)} fusion(bf16[360,1024]{1,0:T(8,128)(2,1)S(1)} %get-tuple-element.128, bf16[1440,256]{1,0:T(8,128)(2,1)S(1)} %pad_maximum_fusion.12, bf16[1440,256]{1,0:T(8,128)(2,1)S(1)} %pad_maximum_fusion.6, bf16[1440,256]{1,0:T(8,128)(2,1)S(1)} %pad_maximum_fusion.16, bf16[1440,256]{1,0:T(8,128)(2,1)S(1)} %pad_maximum_fusion.2), kind=kOutput, calls=%fused_computation.17 | convolution fusion | flops 1073998080 | bytes 4723200 | tf_op jit(solution)/shard_map/dot_general | solution.py:222
  76.5 2.7 %fusion.12 = bf16[1,1440,360]{2,1,0:T(8,128)(2,1)} fusion(bf16[1440,1024]{1,0:T(8,128)(2,1)S(1)} %constant_dynamic-update-slice_fusion, bf16[360,1024]{1,0:T(8,128)(2,1)S(1)} %get-tuple-element.129), kind=kOutput, calls=%fused_computation.12 | convolution fusion | flops 1062201600 | bytes 4723200 | tf_op jit(solution)/shard_map/dot_general | solution.py:221
  79.3 1.6 %collective-permute-done.25 = bf16[360,256]{1,0:T(8,128)(2,1)S(1)} collective-permute-done((bf16[360,256]{1,0:T(8,128)(2,1)S(1)}, bf16[360,256]{1,0:T(8,128)(2,1)S(1)}, u32[]{:S(2)}, u32[]{:S(2)}) %collective-permute-start.25) | collective-permute-done | bytes 184352 | tf_op jit(solution)/shard_map/ppermute | solution.py:104
  80.9 0.8 %fusion.52 = bf16[256,360]{0,1:T(8,128)(2,1)} fusion(bf16[360,256]{1,0:T(8,128)(2,1)S(1)} %collective-permute-done.25, bf16[360,256]{1,0:T(8,128)(2,1)S(1)} %collective-permute-done.24, bf16[360,256]{1,0:T(8,128)(2,1)S(1)} %collective-permute-done.23, bf16[360,256]{1,0:T(8,128)(2,1)S(1)} %constant_dynamic-update-slice_fusion.12, ...), kind=kLoop, calls=%fused_computation.118 | loop fusion | flops 1474560 | bytes 1290244 | tf_op jit(solution)/shard_map/transpose | solution.py:224
  (125 shorter events, 5.4 us)
Async XLA Ops:
  0.6 27.8 %copy-start = (bf16[1,360,1440]{2,1,0:T(8,128)(2,1)S(1)}, bf16[1,360,1440]{2,1,0:T(8,128)(2,1)}, u32[]{:S(2)}) copy-start(bf16[1,360,1440]{2,1,0:T(8,128)(2,1)} %param.13) | copy-start | bytes 3110404
  2.5 21.0 %collective-permute-start.2 = (bf16[736,256]{1,0:T(8,128)(2,1)S(1)}, bf16[736,256]{1,0:T(8,128)(2,1)S(1)}, u32[]{:S(2)}, u32[]{:S(2)}) collective-permute-start(bf16[736,256]{1,0:T(8,128)(2,1)S(1)} %pad_maximum_fusion.17), channel_id=1, source_target_pairs={{0,8},{4,12},{8,0},{12,4},{1,9},{5,13},{9,1},{13,5},{2,10},{6,14},... | collective-permute-start | bytes 1130504 | tf_op jit(solution)/shard_map/ppermute | solution.py:104
  6.6 17.1 %collective-permute-start.1 = (bf16[736,256]{1,0:T(8,128)(2,1)S(1)}, bf16[736,256]{1,0:T(8,128)(2,1)S(1)}, u32[]{:S(2)}, u32[]{:S(2)}) collective-permute-start(bf16[736,256]{1,0:T(8,128)(2,1)S(1)} %pad_maximum_fusion.17), channel_id=1, source_target_pairs={{0,2},{1,3},{2,0},{3,1},{4,6},{5,7},{6,4},{7,5},{8,10},{9,11},{10,... | collective-permute-start | bytes 1130504 | tf_op jit(solution)/shard_map/ppermute | solution.py:104
  8.1 27.2 %collective-permute-start.7 = (bf16[736,256]{1,0:T(8,128)(2,1)S(1)}, bf16[736,256]{1,0:T(8,128)(2,1)S(1)}, u32[]{:S(2)}, u32[]{:S(2)}) collective-permute-start(bf16[736,256]{1,0:T(8,128)(2,1)S(1)} %pad_maximum_fusion.17), channel_id=1, source_target_pairs={{0,4},{4,0},{8,12},{12,8},{1,5},{5,1},{9,13},{13,9},{2,6},{6,2},{1... | collective-permute-start | bytes 1130504 | tf_op jit(solution)/shard_map/ppermute | solution.py:104
  9.7 16.0 %collective-permute-start = (bf16[736,256]{1,0:T(8,128)(2,1)S(1)}, bf16[736,256]{1,0:T(8,128)(2,1)S(1)}, u32[]{:S(2)}, u32[]{:S(2)}) collective-permute-start(bf16[736,256]{1,0:T(8,128)(2,1)S(1)} %pad_maximum_fusion.17), channel_id=1, source_target_pairs={{0,1},{1,0},{2,3},{3,2},{4,5},{5,4},{6,7},{7,6},{8,9},{9,8},{10,11... | collective-permute-start | bytes 1130504 | tf_op jit(solution)/shard_map/ppermute | solution.py:104
  23.7 2.7 %copy-start.1 = (bf16[256,360]{0,1:T(8,128)(2,1)S(1)}, bf16[256,360]{0,1:T(8,128)(2,1)}, u32[]{:S(2)}) copy-start(bf16[256,360]{0,1:T(8,128)(2,1)} %param.8) | copy-start | bytes 552964
  23.7 2.7 %copy-start.2 = (bf16[256,360]{0,1:T(8,128)(2,1)S(1)}, bf16[256,360]{0,1:T(8,128)(2,1)}, u32[]{:S(2)}) copy-start(bf16[256,360]{0,1:T(8,128)(2,1)} %param.7) | copy-start | bytes 552964
  23.8 2.6 %collective-permute-start.3 = (bf16[736,256]{1,0:T(8,128)(2,1)S(1)}, bf16[736,256]{1,0:T(8,128)(2,1)S(1)}, u32[]{:S(2)}, u32[]{:S(2)}) collective-permute-start(bf16[736,256]{1,0:T(8,128)(2,1)S(1)} %constant_dynamic-update-slice_fusion.26), channel_id=1, source_target_pairs={{0,1},{1,0},{2,3},{3,2},{4,5},{5,4},{6,7},{7,6},{8,9},{9,8},{10,11... | collective-permute-start | bytes 1130504 | tf_op jit(solution)/shard_map/ppermute | solution.py:104
  23.9 11.2 %collective-permute-start.5 = (bf16[736,256]{1,0:T(8,128)(2,1)S(1)}, bf16[736,256]{1,0:T(8,128)(2,1)S(1)}, u32[]{:S(2)}, u32[]{:S(2)}) collective-permute-start(bf16[736,256]{1,0:T(8,128)(2,1)S(1)} %collective-permute-done.2), channel_id=1, source_target_pairs={{0,2},{1,3},{2,0},{3,1},{4,6},{5,7},{6,4},{7,5},{8,10},{9,11},{10,... | collective-permute-start | bytes 1130504 | tf_op jit(solution)/shard_map/ppermute | solution.py:104
  25.5 11.9 %collective-permute-start.4 = (bf16[736,256]{1,0:T(8,128)(2,1)S(1)}, bf16[736,256]{1,0:T(8,128)(2,1)S(1)}, u32[]{:S(2)}, u32[]{:S(2)}) collective-permute-start(bf16[736,256]{1,0:T(8,128)(2,1)S(1)} %collective-permute-done.2), channel_id=1, source_target_pairs={{0,1},{1,0},{2,3},{3,2},{4,5},{5,4},{6,7},{7,6},{8,9},{9,8},{10,11... | collective-permute-start | bytes 1130504 | tf_op jit(solution)/shard_map/ppermute | solution.py:104
  25.7 19.1 %collective-permute-start.11 = (bf16[736,256]{1,0:T(8,128)(2,1)S(1)}, bf16[736,256]{1,0:T(8,128)(2,1)S(1)}, u32[]{:S(2)}, u32[]{:S(2)}) collective-permute-start(bf16[736,256]{1,0:T(8,128)(2,1)S(1)} %collective-permute-done.2), channel_id=1, source_target_pairs={{0,4},{4,0},{8,12},{12,8},{1,5},{5,1},{9,13},{13,9},{2,6},{6,2},{1... | collective-permute-start | bytes 1130504 | tf_op jit(solution)/shard_map/ppermute | solution.py:104
  26.6 1.2 %copy-start.3 = (bf16[1,1440,360]{2,1,0:T(8,128)(2,1)S(1)}, bf16[1,1440,360]{2,1,0:T(8,128)(2,1)}, u32[]{:S(2)}) copy-start(bf16[1,1440,360]{2,1,0:T(8,128)(2,1)} %param.11) | copy-start | bytes 3110404
  28.5 1.2 %copy-start.4 = (bf16[1,1440,360]{2,1,0:T(8,128)(2,1)S(1)}, bf16[1,1440,360]{2,1,0:T(8,128)(2,1)}, u32[]{:S(2)}) copy-start(bf16[1,1440,360]{2,1,0:T(8,128)(2,1)} %param.12) | copy-start | bytes 3110404
  35.4 7.2 %collective-permute-start.15 = (bf16[736,256]{1,0:T(8,128)(2,1)S(1)}, bf16[736,256]{1,0:T(8,128)(2,1)S(1)}, u32[]{:S(2)}, u32[]{:S(2)}) collective-permute-start(bf16[736,256]{1,0:T(8,128)(2,1)S(1)} %get-tuple-element.42), channel_id=1, source_target_pairs={{0,1},{1,0},{2,3},{3,2},{4,5},{5,4},{6,7},{7,6},{8,9},{9,8},{10,11... | collective-permute-start | bytes 1130504 | tf_op jit(solution)/shard_map/ppermute | solution.py:104
  35.5 11.2 %collective-permute-start.14 = (bf16[736,256]{1,0:T(8,128)(2,1)S(1)}, bf16[736,256]{1,0:T(8,128)(2,1)S(1)}, u32[]{:S(2)}, u32[]{:S(2)}) collective-permute-start(bf16[736,256]{1,0:T(8,128)(2,1)S(1)} %get-tuple-element.42), channel_id=1, source_target_pairs={{0,2},{1,3},{2,0},{3,1},{4,6},{5,7},{6,4},{7,5},{8,10},{9,11},{10,... | collective-permute-start | bytes 1130504 | tf_op jit(solution)/shard_map/ppermute | solution.py:104
  37.1 1.8 %collective-permute-start.6 = (bf16[736,256]{1,0:T(8,128)(2,1)S(1)}, bf16[736,256]{1,0:T(8,128)(2,1)S(1)}, u32[]{:S(2)}, u32[]{:S(2)}) collective-permute-start(bf16[736,256]{1,0:T(8,128)(2,1)S(1)} %get-tuple-element.44), channel_id=1, source_target_pairs={{0,1},{1,0},{2,3},{3,2},{4,5},{5,4},{6,7},{7,6},{8,9},{9,8},{10,11... | collective-permute-start | bytes 1130504 | tf_op jit(solution)/shard_map/ppermute | solution.py:104
  37.4 11.1 %collective-permute-start.13 = (bf16[736,256]{1,0:T(8,128)(2,1)S(1)}, bf16[736,256]{1,0:T(8,128)(2,1)S(1)}, u32[]{:S(2)}, u32[]{:S(2)}) collective-permute-start(bf16[736,256]{1,0:T(8,128)(2,1)S(1)} %get-tuple-element.44), channel_id=1, source_target_pairs={{0,4},{4,0},{8,12},{12,8},{1,5},{5,1},{9,13},{13,9},{2,6},{6,2},{1... | collective-permute-start | bytes 1130504 | tf_op jit(solution)/shard_map/ppermute | solution.py:104
  42.2 1.8 %collective-permute-start.9 = (bf16[2,360,256]{2,1,0:T(8,128)(2,1)S(1)}, bf16[2,360,256]{2,1,0:T(8,128)(2,1)S(1)}, u32[]{:S(2)}, u32[]{:S(2)}) collective-permute-start(bf16[2,360,256]{2,1,0:T(8,128)(2,1)S(1)} %pad_maximum_fusion.21), channel_id=1, source_target_pairs={{0,1},{1,0},{2,3},{3,2},{4,5},{5,4},{6,7},{7,6},{8,9},{9,8},{10,11... | collective-permute-start | bytes 1105928 | tf_op jit(solution)/shard_map/ppermute | solution.py:104
  42.6 2.0 %collective-permute-start.8 = (bf16[2,360,256]{2,1,0:T(8,128)(2,1)S(1)}, bf16[2,360,256]{2,1,0:T(8,128)(2,1)S(1)}, u32[]{:S(2)}, u32[]{:S(2)}) collective-permute-start(bf16[2,360,256]{2,1,0:T(8,128)(2,1)S(1)} %pad_maximum_fusion.20), channel_id=1, source_target_pairs={{0,1},{1,0},{2,3},{3,2},{4,5},{5,4},{6,7},{7,6},{8,9},{9,8},{10,11... | collective-permute-start | bytes 1105928 | tf_op jit(solution)/shard_map/ppermute | solution.py:104
  44.0 15.6 %collective-permute-start.22 = (bf16[360,256]{1,0:T(8,128)(2,1)S(1)}, bf16[360,256]{1,0:T(8,128)(2,1)S(1)}, u32[]{:S(2)}, u32[]{:S(2)}) collective-permute-start(bf16[360,256]{1,0:T(8,128)(2,1)S(1)} %fusion.46), channel_id=1, source_target_pairs={{0,2},{1,3},{2,0},{3,1},{4,6},{5,7},{6,4},{7,5},{8,10},{9,11},{10,... | collective-permute-start | bytes 552968 | tf_op jit(solution)/shard_map/ppermute | solution.py:104
  44.9 34.3 %collective-permute-start.10 = (bf16[360,256]{1,0:T(8,128)(2,1)S(1)}, bf16[360,256]{1,0:T(8,128)(2,1)S(1)}, u32[]{:S(2)}, u32[]{:S(2)}) collective-permute-start(bf16[360,256]{1,0:T(8,128)(2,1)S(1)} %get-tuple-element.36), channel_id=1, source_target_pairs={{0,2},{1,3},{2,0},{3,1},{4,6},{5,7},{6,4},{7,5},{8,10},{9,11},{10,... | collective-permute-start | bytes 552968 | tf_op jit(solution)/shard_map/ppermute | solution.py:104
  46.4 5.7 %collective-permute-start.12 = (bf16[736,256]{1,0:T(8,128)(2,1)S(1)}, bf16[736,256]{1,0:T(8,128)(2,1)S(1)}, u32[]{:S(2)}, u32[]{:S(2)}) collective-permute-start(bf16[736,256]{1,0:T(8,128)(2,1)S(1)} %get-tuple-element.130), channel_id=1, source_target_pairs={{0,1},{1,0},{2,3},{3,2},{4,5},{5,4},{6,7},{7,6},{8,9},{9,8},{10,11... | collective-permute-start | bytes 1130504 | tf_op jit(solution)/shard_map/ppermute | solution.py:104
  46.7 2.0 %collective-permute-start.16 = (bf16[736,256]{1,0:T(8,128)(2,1)S(1)}, bf16[736,256]{1,0:T(8,128)(2,1)S(1)}, u32[]{:S(2)}, u32[]{:S(2)}) collective-permute-start(bf16[736,256]{1,0:T(8,128)(2,1)S(1)} %get-tuple-element.38), channel_id=1, source_target_pairs={{0,1},{1,0},{2,3},{3,2},{4,5},{5,4},{6,7},{7,6},{8,9},{9,8},{10,11... | collective-permute-start | bytes 1130504 | tf_op jit(solution)/shard_map/ppermute | solution.py:104
  48.6 2.5 %collective-permute-start.17 = (bf16[736,256]{1,0:T(8,128)(2,1)S(1)}, bf16[736,256]{1,0:T(8,128)(2,1)S(1)}, u32[]{:S(2)}, u32[]{:S(2)}) collective-permute-start(bf16[736,256]{1,0:T(8,128)(2,1)S(1)} %get-tuple-element.40), channel_id=1, source_target_pairs={{0,1},{1,0},{2,3},{3,2},{4,5},{5,4},{6,7},{7,6},{8,9},{9,8},{10,11... | collective-permute-start | bytes 1130504 | tf_op jit(solution)/shard_map/ppermute | solution.py:104
  55.5 6.3 %collective-permute-start.20 = (bf16[2,360,256]{2,1,0:T(8,128)(2,1)S(1)}, bf16[2,360,256]{2,1,0:T(8,128)(2,1)S(1)}, u32[]{:S(2)}, u32[]{:S(2)}) collective-permute-start(bf16[2,360,256]{2,1,0:T(8,128)(2,1)S(1)} %pad_maximum_fusion.25), channel_id=1, source_target_pairs={{0,1},{1,0},{2,3},{3,2},{4,5},{5,4},{6,7},{7,6},{8,9},{9,8},{10,11... | collective-permute-start | bytes 1105928 | tf_op jit(solution)/shard_map/ppermute | solution.py:104
  56.1 1.8 %collective-permute-start.18 = (bf16[2,360,256]{2,1,0:T(8,128)(2,1)S(1)}, bf16[2,360,256]{2,1,0:T(8,128)(2,1)S(1)}, u32[]{:S(2)}, u32[]{:S(2)}) collective-permute-start(bf16[2,360,256]{2,1,0:T(8,128)(2,1)S(1)} %pad_maximum_fusion.23), channel_id=1, source_target_pairs={{0,1},{1,0},{2,3},{3,2},{4,5},{5,4},{6,7},{7,6},{8,9},{9,8},{10,11... | collective-permute-start | bytes 1105928 | tf_op jit(solution)/shard_map/ppermute | solution.py:104
  57.9 12.6 %collective-permute-start.19 = (bf16[360,256]{1,0:T(8,128)(2,1)S(1)}, bf16[360,256]{1,0:T(8,128)(2,1)S(1)}, u32[]{:S(2)}, u32[]{:S(2)}) collective-permute-start(bf16[360,256]{1,0:T(8,128)(2,1)S(1)} %fusion.48), channel_id=1, source_target_pairs={{0,2},{1,3},{2,0},{3,1},{4,6},{5,7},{6,4},{7,5},{8,10},{9,11},{10,... | collective-permute-start | bytes 552968 | tf_op jit(solution)/shard_map/ppermute | solution.py:104
  59.9 19.4 %collective-permute-start.24 = (bf16[360,256]{1,0:T(8,128)(2,1)S(1)}, bf16[360,256]{1,0:T(8,128)(2,1)S(1)}, u32[]{:S(2)}, u32[]{:S(2)}) collective-permute-start(bf16[360,256]{1,0:T(8,128)(2,1)S(1)} %fusion.25), channel_id=1, source_target_pairs={{0,8},{4,12},{8,0},{12,4},{1,9},{5,13},{9,1},{13,5},{2,10},{6,14},... | collective-permute-start | bytes 552968 | tf_op jit(solution)/shard_map/ppermute | solution.py:104
  61.8 7.1 %collective-permute-start.21 = (bf16[360,256]{1,0:T(8,128)(2,1)S(1)}, bf16[360,256]{1,0:T(8,128)(2,1)S(1)}, u32[]{:S(2)}, u32[]{:S(2)}) collective-permute-start(bf16[360,256]{1,0:T(8,128)(2,1)S(1)} %fusion.50), channel_id=1, source_target_pairs={{0,2},{1,3},{2,0},{3,1},{4,6},{5,7},{6,4},{7,5},{8,10},{9,11},{10,... | collective-permute-start | bytes 552968 | tf_op jit(solution)/shard_map/ppermute | solution.py:104
  69.0 10.2 %collective-permute-start.23 = (bf16[360,256]{1,0:T(8,128)(2,1)S(1)}, bf16[360,256]{1,0:T(8,128)(2,1)S(1)}, u32[]{:S(2)}, u32[]{:S(2)}) collective-permute-start(bf16[360,256]{1,0:T(8,128)(2,1)S(1)} %fusion.26), channel_id=1, source_target_pairs={{0,4},{4,0},{8,12},{12,8},{1,5},{5,1},{9,13},{13,9},{2,6},{6,2},{1... | collective-permute-start | bytes 552968 | tf_op jit(solution)/shard_map/ppermute | solution.py:104
  70.9 10.1 %collective-permute-start.25 = (bf16[360,256]{1,0:T(8,128)(2,1)S(1)}, bf16[360,256]{1,0:T(8,128)(2,1)S(1)}, u32[]{:S(2)}, u32[]{:S(2)}) collective-permute-start(bf16[360,256]{1,0:T(8,128)(2,1)S(1)} %fusion.27), channel_id=1, source_target_pairs={{0,12},{4,8},{8,4},{12,0},{1,13},{5,9},{9,5},{13,1},{2,14},{6,10},... | collective-permute-start | bytes 552968 | tf_op jit(solution)/shard_map/ppermute | solution.py:104

commit v3 on v2

--- a/solution.py
+++ b/solution.py
@@ -187,39 +187,39 @@
     kept0, sent0 = over_core(kept0, jnp.stack([after(sent0[0], sent2[0]), sent0[1]]))
     kept2, sent2 = over_core(kept2, sent2)
     got2 = swap(sent2, "tensor", 2)
-    sent0 = after(sent0, sent2)
-    got0 = swap(sent0, "tensor", 2)
     z3 = after(z3, sent2)
     near3 = swap(z3, "tensor", 1)
-    far1 = after(far1, sent0)
+    far3 = after(far3, sent2)
+    diagonal3 = swap(far3, "tensor", 1)
+    far1 = after(far1, far3)
     diagonal1 = swap(far1, "tensor", 1)
-    far3 = after(far3, far1)
-    diagonal3 = swap(far3, "tensor", 1)
-    data1, kept1, sent1 = forward(z1, near1, far1, after(diagonal1, far3))
-    kept1, sent1 = over_core(kept1, sent1)
-    got1 = swap(sent1, "tensor", 2)
-    data3, kept3, sent3 = forward(z3, near3, after(far3, data1[3]), diagonal3)
+    data3, kept3, sent3 = forward(z3, near3, far3, diagonal3)
+    data1, kept1, sent1 = forward(z1, near1, far1, after(diagonal1, sent3[0]))
     kept3, sent3 = over_core(kept3, sent3)
     got3 = swap(sent3, "tensor", 2)
+    kept1, sent1 = over_core(kept1, sent1)
     sum2 = add(kept2, after(got2, sent3))
     back2 = swap(sum2, "expert", 2)
-    sum1 = add(kept1, after(got1, sum2))
-    back1 = swap(sum1, "expert", 1)
-    sum3 = add(kept3, after(got3, sum1))
-    back3 = swap(sum3, "expert", 3)
-    got0 = after(got0, sum3)
+    got1 = swap(after(sent1, sum2), "tensor", 2)
 
     parts = lax.optimization_barrier((data0, data1, data2, data3))
 
     def joined(i):
         return jnp.concatenate([p[i] for p in parts], axis=1)
 
+    def product(a, b):
+        return lax.dot_general(a, b, lanes, preferred_element_type=F32).astype(BF16)
+
     x, dy = joined(0), joined(1)
-    grads, scaled = after(joined(2), sum2), after(joined(3), sum3)
-    ups = after(grads[width:], sum3)
-    grad_gate = lax.dot_general(x, grads[:width], lanes, preferred_element_type=F32).astype(BF16)
-    grad_up = lax.dot_general(x, ups, lanes, preferred_element_type=F32).astype(BF16)
-    grad_down = lax.dot_general(scaled, dy, lanes, preferred_element_type=F32).astype(BF16)
+    grads = joined(2)
+    grad_gate = product(x, after(grads[:width], sum2))
+    sum3 = add(kept3, after(got3, grad_gate))
+    back3 = swap(sum3, "expert", 3)
+    sum1 = add(kept1, after(got1, sum3))
+    back1 = swap(sum1, "expert", 1)
+    got0 = swap(after(sent0, sum3), "tensor", 2)
+    grad_up = product(x, after(grads[width:], sum1))
+    grad_down = product(after(joined(3), sum1), dy)
     grad_tokens = add(kept0, got0).astype(F32)
     grad_tokens = (grad_tokens + back1.astype(F32) + back2.astype(F32) + back3.astype(F32)).astype(BF16).T
     return (grad_tokens, grad_gate[None], grad_up[None], grad_down[None])

time: 82 us -> 79.6 us (0.971)
  waiting for transfers between devices: 25.8 us -> 24 us
  matrix products: 18.7 us -> 17.7 us
    ppermute x26, waiting for transfers between devices: 25.8 us -> 24 us  [swap(): return lax.ppermute(block, axis, [(i, i ^ bit) for i in range(size)])]
    dot_general x3, matrix products: 8.42 us -> 7.42 us  [product(): return lax.dot_general(a, b, lanes, preferred_element_type=F32).astype(BF16)]
    unnamed x20 -> x23, local copies, waits for them, and re-layouts: 2.37 us -> 2.39 us
  transfers between devices with their start and end apart: 26 -> 26, of which waited for: 9 -> 8; matrix products, arithmetic and copies ran while one was open for 31% -> 30% of each run, Pallas kernels for 0% -> 0%
where the time goes in v3:
time: 79.6 us; the launch traced here: 79.3 us
  starting transfers between devices  25.3 us (32%)
  waiting for transfers between devices  24 us (30%)
  matrix products  17.7 us (22%)
  other arithmetic  7.17 us (9%)
  local copies, waits for them, and re-layouts  3.67 us (5%)
  between operations  1.46 us (2%)
    ppermute x26, starting transfers between devices, swap(): return lax.ppermute(block, axis, [(i, i ^ bit) for i in range(size)])  25.3 us
    ppermute x26, waiting for transfers between devices, swap(): return lax.ppermute(block, axis, [(i, i ^ bit) for i in range(size)])  24 us
    dot_general x3, matrix products, product(): return lax.dot_general(a, b, lanes, preferred_element_type=F32).astype(BF16)  7.42 us
    dot_general x4, matrix products, forward(): partial = jnp.dot(both, grads, preferred_element_type=F32).astype(BF16)  3.22 us
    dot_general x4, matrix products, forward(): pre_up = lax.dot_general(up, x, first, preferred_element_type=F32)  2.65 us
    unnamed x23, local copies, waits for them, and re-layouts  2.39 us
    dot_general x4, matrix products, forward(): pre_gate = lax.dot_general(gate, x, first, preferred_element_type=F32)  2.34 us
    dot_general x4, matrix products, forward(): hidden_grad = jnp.dot(down, dy, preferred_element_type=F32) * weight  2.04 us
  transfers between devices with their start and end apart: 26, of which 8 were waited for; matrix products, arithmetic and copies ran while one was open for 30% of the time, Pallas kernels for 0%

profile of v3, /device:TPU:0, one launch (start us, length us, event | category | flops | bytes accessed | tf_op | source)
XLA Modules:
  0.0 79.3 jit_solution(8918144458524050297)
XLA Ops:
  0.6 0.8 %fusion.54 = bf16[16,256]{1,0:T(8,128)(2,1)S(1)} fusion(s32[2,256]{1,0:T(2,128)} %bitcast.301, bf16[2,256]{1,0:T(2,128)(2,1)} %bitcast.307), kind=kLoop, calls=%fused_computation.238 | loop fusion | flops 20480 | bytes 11264 | tf_op jit(solution)/shard_map/reduce_sum | solution.py:137
  1.4 1.0 %pad_maximum_fusion.17 = bf16[736,256]{1,0:T(8,128)(2,1)S(1)} fusion(bf16[16,256]{1,0:T(8,128)(2,1)S(1)} %fusion.54, bf16[360,256]{1,0:T(8,128)(2,1)} %bitcast.297, bf16[360,256]{1,0:T(8,128)(2,1)} %bitcast.299), kind=kLoop, calls=%fused_computation.51 | loop fusion | flops 1130496 | bytes 753664 | tf_op jit(solution)/shard_map/concatenate | solution.py:138
  2.5 4.1 %collective-permute-start.2 = (bf16[736,256]{1,0:T(8,128)(2,1)S(1)}, bf16[736,256]{1,0:T(8,128)(2,1)S(1)}, u32[]{:S(2)}, u32[]{:S(2)}) collective-permute-start(bf16[736,256]{1,0:T(8,128)(2,1)S(1)} %pad_maximum_fusion.17), channel_id=1, source_target_pairs={{0,8},{4,12},{8,0},{12,4},{1,9},{5,13},{9,1},{13,5},{2,10},{6,14},... | collective-permute-start | bytes 1130504 | tf_op jit(solution)/shard_map/ppermute | solution.py:104
  6.6 1.5 %collective-permute-start.1 = (bf16[736,256]{1,0:T(8,128)(2,1)S(1)}, bf16[736,256]{1,0:T(8,128)(2,1)S(1)}, u32[]{:S(2)}, u32[]{:S(2)}) collective-permute-start(bf16[736,256]{1,0:T(8,128)(2,1)S(1)} %pad_maximum_fusion.17), channel_id=1, source_target_pairs={{0,2},{1,3},{2,0},{3,1},{4,6},{5,7},{6,4},{7,5},{8,10},{9,11},{10,... | collective-permute-start | bytes 1130504 | tf_op jit(solution)/shard_map/ppermute | solution.py:104
  8.1 1.6 %collective-permute-start.7 = (bf16[736,256]{1,0:T(8,128)(2,1)S(1)}, bf16[736,256]{1,0:T(8,128)(2,1)S(1)}, u32[]{:S(2)}, u32[]{:S(2)}) collective-permute-start(bf16[736,256]{1,0:T(8,128)(2,1)S(1)} %pad_maximum_fusion.17), channel_id=1, source_target_pairs={{0,4},{4,0},{8,12},{12,8},{1,5},{5,1},{9,13},{13,9},{2,6},{6,2},{1... | collective-permute-start | bytes 1130504 | tf_op jit(solution)/shard_map/ppermute | solution.py:104
  9.7 13.9 %collective-permute-done.2 = bf16[736,256]{1,0:T(8,128)(2,1)S(1)} collective-permute-done((bf16[736,256]{1,0:T(8,128)(2,1)S(1)}, bf16[736,256]{1,0:T(8,128)(2,1)S(1)}, u32[]{:S(2)}, u32[]{:S(2)}) %collective-permute-start.2) | collective-permute-done | bytes 376864 | tf_op jit(solution)/shard_map/ppermute | solution.py:104
  23.5 0.1 fusion.57
  23.8 1.6 %collective-permute-start.5 = (bf16[736,256]{1,0:T(8,128)(2,1)S(1)}, bf16[736,256]{1,0:T(8,128)(2,1)S(1)}, u32[]{:S(2)}, u32[]{:S(2)}) collective-permute-start(bf16[736,256]{1,0:T(8,128)(2,1)S(1)} %collective-permute-done.2), channel_id=1, source_target_pairs={{0,2},{1,3},{2,0},{3,1},{4,6},{5,7},{6,4},{7,5},{8,10},{9,11},{10,... | collective-permute-start | bytes 1130504 | tf_op jit(solution)/shard_map/ppermute | solution.py:104
  25.4 0.2 collective-permute-start.4
  25.7 0.7 collective-permute-start.9
  26.5 0.2 pad_maximum_fusion.1
  26.8 1.1 %copy-done.4 = bf16[1,1440,360]{2,1,0:T(8,128)(2,1)S(1)} copy-done((bf16[1,1440,360]{2,1,0:T(8,128)(2,1)S(1)}, bf16[1,1440,360]{2,1,0:T(8,128)(2,1)}, u32[]{:S(2)}) %copy-start.4) | copy-done | bytes 1036824
  27.9 0.6 convolution_bitcast_fusion.6
  28.5 0.5 fusion.15
  29.0 0.8 copy-done.5
  29.8 0.7 multiply_convert_fusion.3
  30.4 0.8 %convolution_convert_fusion.5 = bf16[1440,256]{1,0:T(8,128)(2,1)S(1)} fusion(bf16[360,256]{1,0:T(8,128)(2,1)S(1)} %get-tuple-element.79, bf16[360,256]{1,0:T(8,128)(2,1)S(1)} %get-tuple-element.78, bf16[1440,360]{1,0:T(8,128)(2,1)S(1)} %bitcast.313, bf16[1440,360]{1,0:T(8,128)(2,1)S(1)} %bitcast.309), kind=kOutput, calls=%fused_computation.15 | convolution fusion | flops 536094720 | bytes 3179520 | tf_op jit(solution)/shard_map/dot_general | solution.py:161
  31.3 0.1 fusion.58
  31.4 3.7 %collective-permute-done.5 = bf16[736,256]{1,0:T(8,128)(2,1)S(1)} collective-permute-done((bf16[736,256]{1,0:T(8,128)(2,1)S(1)}, bf16[736,256]{1,0:T(8,128)(2,1)S(1)}, u32[]{:S(2)}, u32[]{:S(2)}) %collective-permute-start.5) | collective-permute-done | bytes 376864 | tf_op jit(solution)/shard_map/ppermute | solution.py:104
  35.1 0.7 collective-permute-start.12
  35.8 0.1 fusion.59
  36.0 1.5 %collective-permute-start.17 = (bf16[736,256]{1,0:T(8,128)(2,1)S(1)}, bf16[736,256]{1,0:T(8,128)(2,1)S(1)}, u32[]{:S(2)}, u32[]{:S(2)}) collective-permute-start(bf16[736,256]{1,0:T(8,128)(2,1)S(1)} %get-tuple-element.48), channel_id=1, source_target_pairs={{0,2},{1,3},{2,0},{3,1},{4,6},{5,7},{6,4},{7,5},{8,10},{9,11},{10,... | collective-permute-start | bytes 1130504 | tf_op jit(solution)/shard_map/ppermute | solution.py:104
  37.5 0.1 fusion.60
  37.7 0.3 collective-permute-start.16
  38.4 0.6 convolution_bitcast_fusion.4
  39.3 0.5 fusion.20
  39.8 0.7 multiply_convert_fusion.1
  40.5 0.8 %convolution_convert_fusion.4 = bf16[1440,256]{1,0:T(8,128)(2,1)S(1)} fusion(bf16[360,256]{1,0:T(8,128)(2,1)S(1)} %get-tuple-element.61, bf16[360,256]{1,0:T(8,128)(2,1)S(1)} %get-tuple-element.60, bf16[1440,360]{1,0:T(8,128)(2,1)S(1)} %bitcast.314, bf16[1440,360]{1,0:T(8,128)(2,1)S(1)} %bitcast.310), kind=kOutput, calls=%fused_computation.14 | convolution fusion | flops 536094720 | bytes 3179520 | tf_op jit(solution)/shard_map/dot_general | solution.py:161
  41.4 0.3 collective-permute-start.10
  41.7 0.1 fusion.61
  42.0 0.3 collective-permute-start.8
  42.3 0.8 %collective-permute-done.10 = bf16[2,360,256]{2,1,0:T(8,128)(2,1)S(1)} collective-permute-done((bf16[2,360,256]{2,1,0:T(8,128)(2,1)S(1)}, bf16[2,360,256]{2,1,0:T(8,128)(2,1)S(1)}, u32[]{:S(2)}, u32[]{:S(2)}) %collective-permute-start.10) | collective-permute-done | bytes 368672 | tf_op jit(solution)/shard_map/ppermute | solution.py:104
  43.2 0.1 fusion.62
  43.3 2.2 %collective-permute-done.12 = bf16[736,256]{1,0:T(8,128)(2,1)S(1)} collective-permute-done((bf16[736,256]{1,0:T(8,128)(2,1)S(1)}, bf16[736,256]{1,0:T(8,128)(2,1)S(1)}, u32[]{:S(2)}, u32[]{:S(2)}) %collective-permute-start.12) | collective-permute-done | bytes 376864 | tf_op jit(solution)/shard_map/ppermute | solution.py:104
  45.6 0.5 collective-permute-start.11
  46.1 0.1 fusion.63
  46.2 1.0 %collective-permute-done.17 = bf16[736,256]{1,0:T(8,128)(2,1)S(1)} collective-permute-done((bf16[736,256]{1,0:T(8,128)(2,1)S(1)}, bf16[736,256]{1,0:T(8,128)(2,1)S(1)}, u32[]{:S(2)}, u32[]{:S(2)}) %collective-permute-start.17) | collective-permute-done | bytes 376864 | tf_op jit(solution)/shard_map/ppermute | solution.py:104
  47.3 1.6 %collective-permute-start.19 = (bf16[360,256]{1,0:T(8,128)(2,1)S(1)}, bf16[360,256]{1,0:T(8,128)(2,1)S(1)}, u32[]{:S(2)}, u32[]{:S(2)}) collective-permute-start(bf16[360,256]{1,0:T(8,128)(2,1)S(1)} %fusion.44), channel_id=1, source_target_pairs={{0,2},{1,3},{2,0},{3,1},{4,6},{5,7},{6,4},{7,5},{8,10},{9,11},{10,... | collective-permute-start | bytes 552968 | tf_op jit(solution)/shard_map/ppermute | solution.py:104
  49.4 0.6 convolution_bitcast_fusion.2
  50.0 0.5 fusion.18
  50.5 0.7 multiply_convert_fusion
  51.2 0.8 %convolution_convert_fusion.3 = bf16[1440,256]{1,0:T(8,128)(2,1)S(1)} fusion(bf16[360,256]{1,0:T(8,128)(2,1)S(1)} %get-tuple-element.58, bf16[360,256]{1,0:T(8,128)(2,1)S(1)} %get-tuple-element.57, bf16[1440,360]{1,0:T(8,128)(2,1)S(1)} %bitcast.315, bf16[1440,360]{1,0:T(8,128)(2,1)S(1)} %bitcast.311), kind=kOutput, calls=%fused_computation.13 | convolution fusion | flops 536094720 | bytes 3179520 | tf_op jit(solution)/shard_map/dot_general | solution.py:161
  52.0 0.1 fusion.64
  52.5 0.6 convolution_bitcast_fusion
  53.3 0.6 fusion.16
  54.1 0.7 multiply_convert_fusion.2
  54.8 0.8 %convolution_convert_fusion.2 = bf16[1440,256]{1,0:T(8,128)(2,1)S(1)} fusion(bf16[360,256]{1,0:T(8,128)(2,1)S(1)} %get-tuple-element.64, bf16[360,256]{1,0:T(8,128)(2,1)S(1)} %get-tuple-element.63, bf16[1440,360]{1,0:T(8,128)(2,1)S(1)} %bitcast.316, bf16[1440,360]{1,0:T(8,128)(2,1)S(1)} %bitcast.312), kind=kOutput, calls=%fused_computation.12 | convolution fusion | flops 536094720 | bytes 3179520 | tf_op jit(solution)/shard_map/dot_general | solution.py:161
  55.7 0.3 collective-permute-start.14
  56.2 0.3 collective-permute-start.21
  57.1 0.1 fusion.83
  57.2 0.2 collective-permute-done.14
  57.5 0.6 collective-permute-start.15
  58.4 3.5 %collective-permute-start.24 = (bf16[360,256]{1,0:T(8,128)(2,1)S(1)}, bf16[360,256]{1,0:T(8,128)(2,1)S(1)}, u32[]{:S(2)}, u32[]{:S(2)}) collective-permute-start(bf16[360,256]{1,0:T(8,128)(2,1)S(1)} %fusion.24), channel_id=1, source_target_pairs={{0,8},{4,12},{8,0},{12,4},{1,9},{5,13},{9,1},{13,5},{2,10},{6,14},... | collective-permute-start | bytes 552968 | tf_op jit(solution)/shard_map/ppermute | solution.py:104
  62.2 1.5 %collective-permute-start.22 = (bf16[360,256]{1,0:T(8,128)(2,1)S(1)}, bf16[360,256]{1,0:T(8,128)(2,1)S(1)}, u32[]{:S(2)}, u32[]{:S(2)}) collective-permute-start(bf16[360,256]{1,0:T(8,128)(2,1)S(1)} %constant_dynamic-update-slice_fusion.13), channel_id=1, source_target_pairs={{0,2},{1,3},{2,0},{3,1},{4,6},{5,7},{6,4},{7,5},{8,10},{9,11},{10,... | collective-permute-start | bytes 552968 | tf_op jit(solution)/shard_map/ppermute | solution.py:104
  63.7 1.7 %convolution_convert_fusion.1 = bf16[1440,360]{1,0:T(8,128)(2,1)S(1)} fusion(bf16[1440,1024]{1,0:T(8,128)(2,1)S(1)} %constant_dynamic-update-slice_fusion, bf16[360,1024]{1,0:T(8,128)(2,1)S(1)} %fusion.50), kind=kOutput, calls=%fused_computation.9 | convolution fusion | flops 1062201600 | bytes 4723200 | tf_op jit(solution)/shard_map/dot_general | solution.py:211
  65.5 0.1 fusion.67
  65.8 2.4 %collective-permute-start.25 = (bf16[360,256]{1,0:T(8,128)(2,1)S(1)}, bf16[360,256]{1,0:T(8,128)(2,1)S(1)}, u32[]{:S(2)}, u32[]{:S(2)}) collective-permute-start(bf16[360,256]{1,0:T(8,128)(2,1)S(1)} %fusion.25), channel_id=1, source_target_pairs={{0,12},{4,8},{8,4},{12,0},{1,13},{5,9},{9,5},{13,1},{2,14},{6,10},... | collective-permute-start | bytes 552968 | tf_op jit(solution)/shard_map/ppermute | solution.py:104
  68.3 0.2 collective-permute-done.22
  68.6 1.3 %collective-permute-start.23 = (bf16[360,256]{1,0:T(8,128)(2,1)S(1)}, bf16[360,256]{1,0:T(8,128)(2,1)S(1)}, u32[]{:S(2)}, u32[]{:S(2)}) collective-permute-start(bf16[360,256]{1,0:T(8,128)(2,1)S(1)} %fusion.23), channel_id=1, source_target_pairs={{0,4},{4,0},{8,12},{12,8},{1,5},{5,1},{9,13},{13,9},{2,6},{6,2},{1... | collective-permute-start | bytes 552968 | tf_op jit(solution)/shard_map/ppermute | solution.py:104
  70.0 0.5 collective-permute-start.20
  70.7 3.0 %fusion.12 = bf16[1,360,1440]{2,1,0:T(8,128)(2,1)} fusion(bf16[360,1024]{1,0:T(8,128)(2,1)S(1)} %get-tuple-element.138, bf16[1440,256]{1,0:T(8,128)(2,1)S(1)} %pad_maximum_fusion.10, bf16[1440,256]{1,0:T(8,128)(2,1)S(1)} %pad_maximum_fusion.6, bf16[1440,256]{1,0:T(8,128)(2,1)S(1)} %pad_maximum_fusion.16, bf16[1440,256]{1,0:T(8,128)(2,1)S(1)} %pad_maximum_fusion.2), kind=kOutput, calls=%fused_computation.16 | convolution fusion | flops 1073998080 | bytes 4723200 | tf_op jit(solution)/shard_map/dot_general | solution.py:211
  73.6 2.7 %fusion.11 = bf16[1,1440,360]{2,1,0:T(8,128)(2,1)} fusion(bf16[1440,1024]{1,0:T(8,128)(2,1)S(1)} %constant_dynamic-update-slice_fusion, bf16[360,1024]{1,0:T(8,128)(2,1)S(1)} %get-tuple-element.139), kind=kOutput, calls=%fused_computation.11 | convolution fusion | flops 1062201600 | bytes 4723200 | tf_op jit(solution)/shard_map/dot_general | solution.py:211
  76.4 2.1 %collective-permute-done.23 = bf16[360,256]{1,0:T(8,128)(2,1)S(1)} collective-permute-done((bf16[360,256]{1,0:T(8,128)(2,1)S(1)}, bf16[360,256]{1,0:T(8,128)(2,1)S(1)}, u32[]{:S(2)}, u32[]{:S(2)}) %collective-permute-start.23) | collective-permute-done | bytes 184352 | tf_op jit(solution)/shard_map/ppermute | solution.py:104
  78.5 0.8 %fusion.49 = bf16[256,360]{0,1:T(8,128)(2,1)} fusion(bf16[360,256]{1,0:T(8,128)(2,1)S(1)} %collective-permute-done.25, bf16[360,256]{1,0:T(8,128)(2,1)S(1)} %collective-permute-done.24, bf16[360,256]{1,0:T(8,128)(2,1)S(1)} %collective-permute-done.23, bf16[360,256]{1,0:T(8,128)(2,1)S(1)} %collective-permute-done.20, ...), kind=kLoop, calls=%fused_computation.115 | loop fusion | flops 1474560 | bytes 1290244 | tf_op jit(solution)/shard_map/transpose | solution.py:224
  (125 shorter events, 5.1 us)
Async XLA Ops:
  0.6 27.9 %copy-start = (bf16[1,360,1440]{2,1,0:T(8,128)(2,1)S(1)}, bf16[1,360,1440]{2,1,0:T(8,128)(2,1)}, u32[]{:S(2)}) copy-start(bf16[1,360,1440]{2,1,0:T(8,128)(2,1)} %param.13) | copy-start | bytes 3110404
  2.5 21.0 %collective-permute-start.2 = (bf16[736,256]{1,0:T(8,128)(2,1)S(1)}, bf16[736,256]{1,0:T(8,128)(2,1)S(1)}, u32[]{:S(2)}, u32[]{:S(2)}) collective-permute-start(bf16[736,256]{1,0:T(8,128)(2,1)S(1)} %pad_maximum_fusion.17), channel_id=1, source_target_pairs={{0,8},{4,12},{8,0},{12,4},{1,9},{5,13},{9,1},{13,5},{2,10},{6,14},... | collective-permute-start | bytes 1130504 | tf_op jit(solution)/shard_map/ppermute | solution.py:104
  6.6 17.1 %collective-permute-start.1 = (bf16[736,256]{1,0:T(8,128)(2,1)S(1)}, bf16[736,256]{1,0:T(8,128)(2,1)S(1)}, u32[]{:S(2)}, u32[]{:S(2)}) collective-permute-start(bf16[736,256]{1,0:T(8,128)(2,1)S(1)} %pad_maximum_fusion.17), channel_id=1, source_target_pairs={{0,2},{1,3},{2,0},{3,1},{4,6},{5,7},{6,4},{7,5},{8,10},{9,11},{10,... | collective-permute-start | bytes 1130504 | tf_op jit(solution)/shard_map/ppermute | solution.py:104
  8.1 17.6 %collective-permute-start = (bf16[736,256]{1,0:T(8,128)(2,1)S(1)}, bf16[736,256]{1,0:T(8,128)(2,1)S(1)}, u32[]{:S(2)}, u32[]{:S(2)}) collective-permute-start(bf16[736,256]{1,0:T(8,128)(2,1)S(1)} %pad_maximum_fusion.17), channel_id=1, source_target_pairs={{0,1},{1,0},{2,3},{3,2},{4,5},{5,4},{6,7},{7,6},{8,9},{9,8},{10,11... | collective-permute-start | bytes 1130504 | tf_op jit(solution)/shard_map/ppermute | solution.py:104
  8.1 27.8 %collective-permute-start.7 = (bf16[736,256]{1,0:T(8,128)(2,1)S(1)}, bf16[736,256]{1,0:T(8,128)(2,1)S(1)}, u32[]{:S(2)}, u32[]{:S(2)}) collective-permute-start(bf16[736,256]{1,0:T(8,128)(2,1)S(1)} %pad_maximum_fusion.17), channel_id=1, source_target_pairs={{0,4},{4,0},{8,12},{12,8},{1,5},{5,1},{9,13},{13,9},{2,6},{6,2},{1... | collective-permute-start | bytes 1130504 | tf_op jit(solution)/shard_map/ppermute | solution.py:104
  23.7 2.7 %copy-start.1 = (bf16[256,360]{0,1:T(8,128)(2,1)S(1)}, bf16[256,360]{0,1:T(8,128)(2,1)}, u32[]{:S(2)}) copy-start(bf16[256,360]{0,1:T(8,128)(2,1)} %param.8) | copy-start | bytes 552964
  23.7 2.7 %copy-start.2 = (bf16[256,360]{0,1:T(8,128)(2,1)S(1)}, bf16[256,360]{0,1:T(8,128)(2,1)}, u32[]{:S(2)}) copy-start(bf16[256,360]{0,1:T(8,128)(2,1)} %param.7) | copy-start | bytes 552964
  23.7 2.7 %collective-permute-start.3 = (bf16[736,256]{1,0:T(8,128)(2,1)S(1)}, bf16[736,256]{1,0:T(8,128)(2,1)S(1)}, u32[]{:S(2)}, u32[]{:S(2)}) collective-permute-start(bf16[736,256]{1,0:T(8,128)(2,1)S(1)} %constant_dynamic-update-slice_fusion.25), channel_id=1, source_target_pairs={{0,1},{1,0},{2,3},{3,2},{4,5},{5,4},{6,7},{7,6},{8,9},{9,8},{10,11... | collective-permute-start | bytes 1130504 | tf_op jit(solution)/shard_map/ppermute | solution.py:104
  23.8 11.2 %collective-permute-start.5 = (bf16[736,256]{1,0:T(8,128)(2,1)S(1)}, bf16[736,256]{1,0:T(8,128)(2,1)S(1)}, u32[]{:S(2)}, u32[]{:S(2)}) collective-permute-start(bf16[736,256]{1,0:T(8,128)(2,1)S(1)} %collective-permute-done.2), channel_id=1, source_target_pairs={{0,2},{1,3},{2,0},{3,1},{4,6},{5,7},{6,4},{7,5},{8,10},{9,11},{10,... | collective-permute-start | bytes 1130504 | tf_op jit(solution)/shard_map/ppermute | solution.py:104
  25.4 12.3 %collective-permute-start.4 = (bf16[736,256]{1,0:T(8,128)(2,1)S(1)}, bf16[736,256]{1,0:T(8,128)(2,1)S(1)}, u32[]{:S(2)}, u32[]{:S(2)}) collective-permute-start(bf16[736,256]{1,0:T(8,128)(2,1)S(1)} %collective-permute-done.2), channel_id=1, source_target_pairs={{0,1},{1,0},{2,3},{3,2},{4,5},{5,4},{6,7},{7,6},{8,9},{9,8},{10,11... | collective-permute-start | bytes 1130504 | tf_op jit(solution)/shard_map/ppermute | solution.py:104
  25.7 17.6 %collective-permute-start.9 = (bf16[736,256]{1,0:T(8,128)(2,1)S(1)}, bf16[736,256]{1,0:T(8,128)(2,1)S(1)}, u32[]{:S(2)}, u32[]{:S(2)}) collective-permute-start(bf16[736,256]{1,0:T(8,128)(2,1)S(1)} %collective-permute-done.2), channel_id=1, source_target_pairs={{0,4},{4,0},{8,12},{12,8},{1,5},{5,1},{9,13},{13,9},{2,6},{6,2},{1... | collective-permute-start | bytes 1130504 | tf_op jit(solution)/shard_map/ppermute | solution.py:104
  26.7 1.2 %copy-start.4 = (bf16[1,1440,360]{2,1,0:T(8,128)(2,1)S(1)}, bf16[1,1440,360]{2,1,0:T(8,128)(2,1)}, u32[]{:S(2)}) copy-start(bf16[1,1440,360]{2,1,0:T(8,128)(2,1)} %param.11) | copy-start | bytes 3110404
  28.5 1.2 %copy-start.5 = (bf16[1,1440,360]{2,1,0:T(8,128)(2,1)S(1)}, bf16[1,1440,360]{2,1,0:T(8,128)(2,1)}, u32[]{:S(2)}) copy-start(bf16[1,1440,360]{2,1,0:T(8,128)(2,1)} %param.12) | copy-start | bytes 3110404
  35.1 10.4 %collective-permute-start.12 = (bf16[736,256]{1,0:T(8,128)(2,1)S(1)}, bf16[736,256]{1,0:T(8,128)(2,1)S(1)}, u32[]{:S(2)}, u32[]{:S(2)}) collective-permute-start(bf16[736,256]{1,0:T(8,128)(2,1)S(1)} %get-tuple-element.52), channel_id=1, source_target_pairs={{0,4},{4,0},{8,12},{12,8},{1,5},{5,1},{9,13},{13,9},{2,6},{6,2},{1... | collective-permute-start | bytes 1130504 | tf_op jit(solution)/shard_map/ppermute | solution.py:104
  35.8 2.4 %collective-permute-start.6 = (bf16[736,256]{1,0:T(8,128)(2,1)S(1)}, bf16[736,256]{1,0:T(8,128)(2,1)S(1)}, u32[]{:S(2)}, u32[]{:S(2)}) collective-permute-start(bf16[736,256]{1,0:T(8,128)(2,1)S(1)} %get-tuple-element.52), channel_id=1, source_target_pairs={{0,1},{1,0},{2,3},{3,2},{4,5},{5,4},{6,7},{7,6},{8,9},{9,8},{10,11... | collective-permute-start | bytes 1130504 | tf_op jit(solution)/shard_map/ppermute | solution.py:104
  36.0 11.2 %collective-permute-start.17 = (bf16[736,256]{1,0:T(8,128)(2,1)S(1)}, bf16[736,256]{1,0:T(8,128)(2,1)S(1)}, u32[]{:S(2)}, u32[]{:S(2)}) collective-permute-start(bf16[736,256]{1,0:T(8,128)(2,1)S(1)} %get-tuple-element.48), channel_id=1, source_target_pairs={{0,2},{1,3},{2,0},{3,1},{4,6},{5,7},{6,4},{7,5},{8,10},{9,11},{10,... | collective-permute-start | bytes 1130504 | tf_op jit(solution)/shard_map/ppermute | solution.py:104
  37.7 4.3 %collective-permute-start.16 = (bf16[736,256]{1,0:T(8,128)(2,1)S(1)}, bf16[736,256]{1,0:T(8,128)(2,1)S(1)}, u32[]{:S(2)}, u32[]{:S(2)}) collective-permute-start(bf16[736,256]{1,0:T(8,128)(2,1)S(1)} %get-tuple-element.48), channel_id=1, source_target_pairs={{0,1},{1,0},{2,3},{3,2},{4,5},{5,4},{6,7},{7,6},{8,9},{9,8},{10,11... | collective-permute-start | bytes 1130504 | tf_op jit(solution)/shard_map/ppermute | solution.py:104
  41.4 1.8 %collective-permute-start.10 = (bf16[2,360,256]{2,1,0:T(8,128)(2,1)S(1)}, bf16[2,360,256]{2,1,0:T(8,128)(2,1)S(1)}, u32[]{:S(2)}, u32[]{:S(2)}) collective-permute-start(bf16[2,360,256]{2,1,0:T(8,128)(2,1)S(1)} %pad_maximum_fusion.21), channel_id=1, source_target_pairs={{0,1},{1,0},{2,3},{3,2},{4,5},{5,4},{6,7},{7,6},{8,9},{9,8},{10,11... | collective-permute-start | bytes 1105928 | tf_op jit(solution)/shard_map/ppermute | solution.py:104
  42.0 6.9 %collective-permute-start.8 = (bf16[2,360,256]{2,1,0:T(8,128)(2,1)S(1)}, bf16[2,360,256]{2,1,0:T(8,128)(2,1)S(1)}, u32[]{:S(2)}, u32[]{:S(2)}) collective-permute-start(bf16[2,360,256]{2,1,0:T(8,128)(2,1)S(1)} %pad_maximum_fusion.20), channel_id=1, source_target_pairs={{0,1},{1,0},{2,3},{3,2},{4,5},{5,4},{6,7},{7,6},{8,9},{9,8},{10,11... | collective-permute-start | bytes 1105928 | tf_op jit(solution)/shard_map/ppermute | solution.py:104
  45.6 3.4 %collective-permute-start.13 = (bf16[736,256]{1,0:T(8,128)(2,1)S(1)}, bf16[736,256]{1,0:T(8,128)(2,1)S(1)}, u32[]{:S(2)}, u32[]{:S(2)}) collective-permute-start(bf16[736,256]{1,0:T(8,128)(2,1)S(1)} %get-tuple-element.50), channel_id=1, source_target_pairs={{0,1},{1,0},{2,3},{3,2},{4,5},{5,4},{6,7},{7,6},{8,9},{9,8},{10,11... | collective-permute-start | bytes 1130504 | tf_op jit(solution)/shard_map/ppermute | solution.py:104
  45.6 3.5 %collective-permute-start.11 = (bf16[736,256]{1,0:T(8,128)(2,1)S(1)}, bf16[736,256]{1,0:T(8,128)(2,1)S(1)}, u32[]{:S(2)}, u32[]{:S(2)}) collective-permute-start(bf16[736,256]{1,0:T(8,128)(2,1)S(1)} %get-tuple-element.142), channel_id=1, source_target_pairs={{0,1},{1,0},{2,3},{3,2},{4,5},{5,4},{6,7},{7,6},{8,9},{9,8},{10,11... | collective-permute-start | bytes 1130504 | tf_op jit(solution)/shard_map/ppermute | solution.py:104
  47.3 4.9 %collective-permute-start.18 = (bf16[736,256]{1,0:T(8,128)(2,1)S(1)}, bf16[736,256]{1,0:T(8,128)(2,1)S(1)}, u32[]{:S(2)}, u32[]{:S(2)}) collective-permute-start(bf16[736,256]{1,0:T(8,128)(2,1)S(1)} %constant_dynamic-update-slice_fusion.18), channel_id=1, source_target_pairs={{0,1},{1,0},{2,3},{3,2},{4,5},{5,4},{6,7},{7,6},{8,9},{9,8},{10,11... | collective-permute-start | bytes 1130504 | tf_op jit(solution)/shard_map/ppermute | solution.py:104
  47.3 10.9 %collective-permute-start.19 = (bf16[360,256]{1,0:T(8,128)(2,1)S(1)}, bf16[360,256]{1,0:T(8,128)(2,1)S(1)}, u32[]{:S(2)}, u32[]{:S(2)}) collective-permute-start(bf16[360,256]{1,0:T(8,128)(2,1)S(1)} %fusion.44), channel_id=1, source_target_pairs={{0,2},{1,3},{2,0},{3,1},{4,6},{5,7},{6,4},{7,5},{8,10},{9,11},{10,... | collective-permute-start | bytes 552968 | tf_op jit(solution)/shard_map/ppermute | solution.py:104
  55.7 1.8 %collective-permute-start.14 = (bf16[2,360,256]{2,1,0:T(8,128)(2,1)S(1)}, bf16[2,360,256]{2,1,0:T(8,128)(2,1)S(1)}, u32[]{:S(2)}, u32[]{:S(2)}) collective-permute-start(bf16[2,360,256]{2,1,0:T(8,128)(2,1)S(1)} %pad_maximum_fusion.23), channel_id=1, source_target_pairs={{0,1},{1,0},{2,3},{3,2},{4,5},{5,4},{6,7},{7,6},{8,9},{9,8},{10,11... | collective-permute-start | bytes 1105928 | tf_op jit(solution)/shard_map/ppermute | solution.py:104
  56.2 5.8 %collective-permute-start.21 = (bf16[2,360,256]{2,1,0:T(8,128)(2,1)S(1)}, bf16[2,360,256]{2,1,0:T(8,128)(2,1)S(1)}, u32[]{:S(2)}, u32[]{:S(2)}) collective-permute-start(bf16[2,360,256]{2,1,0:T(8,128)(2,1)S(1)} %pad_maximum_fusion.25), channel_id=1, source_target_pairs={{0,1},{1,0},{2,3},{3,2},{4,5},{5,4},{6,7},{7,6},{8,9},{9,8},{10,11... | collective-permute-start | bytes 1105928 | tf_op jit(solution)/shard_map/ppermute | solution.py:104
  57.5 8.1 %collective-permute-start.15 = (bf16[360,256]{1,0:T(8,128)(2,1)S(1)}, bf16[360,256]{1,0:T(8,128)(2,1)S(1)}, u32[]{:S(2)}, u32[]{:S(2)}) collective-permute-start(bf16[360,256]{1,0:T(8,128)(2,1)S(1)} %fusion.46), channel_id=1, source_target_pairs={{0,2},{1,3},{2,0},{3,1},{4,6},{5,7},{6,4},{7,5},{8,10},{9,11},{10,... | collective-permute-start | bytes 552968 | tf_op jit(solution)/shard_map/ppermute | solution.py:104
  58.4 18.0 %collective-permute-start.24 = (bf16[360,256]{1,0:T(8,128)(2,1)S(1)}, bf16[360,256]{1,0:T(8,128)(2,1)S(1)}, u32[]{:S(2)}, u32[]{:S(2)}) collective-permute-start(bf16[360,256]{1,0:T(8,128)(2,1)S(1)} %fusion.24), channel_id=1, source_target_pairs={{0,8},{4,12},{8,0},{12,4},{1,9},{5,13},{9,1},{13,5},{2,10},{6,14},... | collective-permute-start | bytes 552968 | tf_op jit(solution)/shard_map/ppermute | solution.py:104
  62.2 6.2 %collective-permute-start.22 = (bf16[360,256]{1,0:T(8,128)(2,1)S(1)}, bf16[360,256]{1,0:T(8,128)(2,1)S(1)}, u32[]{:S(2)}, u32[]{:S(2)}) collective-permute-start(bf16[360,256]{1,0:T(8,128)(2,1)S(1)} %constant_dynamic-update-slice_fusion.13), channel_id=1, source_target_pairs={{0,2},{1,3},{2,0},{3,1},{4,6},{5,7},{6,4},{7,5},{8,10},{9,11},{10,... | collective-permute-start | bytes 552968 | tf_op jit(solution)/shard_map/ppermute | solution.py:104
  65.5 8.1 %copy-start.3 = (bf16[1440,360]{1,0:T(8,128)(2,1)}, bf16[1440,360]{1,0:T(8,128)(2,1)S(1)}, u32[]{:S(2)}) copy-start(bf16[1440,360]{1,0:T(8,128)(2,1)S(1)} %convolution_convert_fusion.1) | copy-start | bytes 3110404
  65.8 10.6 %collective-permute-start.25 = (bf16[360,256]{1,0:T(8,128)(2,1)S(1)}, bf16[360,256]{1,0:T(8,128)(2,1)S(1)}, u32[]{:S(2)}, u32[]{:S(2)}) collective-permute-start(bf16[360,256]{1,0:T(8,128)(2,1)S(1)} %fusion.25), channel_id=1, source_target_pairs={{0,12},{4,8},{8,4},{12,0},{1,13},{5,9},{9,5},{13,1},{2,14},{6,10},... | collective-permute-start | bytes 552968 | tf_op jit(solution)/shard_map/ppermute | solution.py:104
  68.6 9.9 %collective-permute-start.23 = (bf16[360,256]{1,0:T(8,128)(2,1)S(1)}, bf16[360,256]{1,0:T(8,128)(2,1)S(1)}, u32[]{:S(2)}, u32[]{:S(2)}) collective-permute-start(bf16[360,256]{1,0:T(8,128)(2,1)S(1)} %fusion.23), channel_id=1, source_target_pairs={{0,4},{4,0},{8,12},{12,8},{1,5},{5,1},{9,13},{13,9},{2,6},{6,2},{1... | collective-permute-start | bytes 552968 | tf_op jit(solution)/shard_map/ppermute | solution.py:104
  70.0 8.4 %collective-permute-start.20 = (bf16[360,256]{1,0:T(8,128)(2,1)S(1)}, bf16[360,256]{1,0:T(8,128)(2,1)S(1)}, u32[]{:S(2)}, u32[]{:S(2)}) collective-permute-start(bf16[360,256]{1,0:T(8,128)(2,1)S(1)} %get-tuple-element.140), channel_id=1, source_target_pairs={{0,2},{1,3},{2,0},{3,1},{4,6},{5,7},{6,4},{7,5},{8,10},{9,11},{10,... | collective-permute-start | bytes 552968 | tf_op jit(solution)/shard_map/ppermute | solution.py:104
